TPU v7x, 32 devices: a whole 2x2x4 slice. The times are simulated.
32 devices in a mesh: section: 2 (over core), dp: 16 (over z, y, x).
Axes of the slice: x: 2, y: 2, z: 4, core: 2. Of those that a mesh axis runs over, the one named last changes fastest.
Arguments:
- stream_pair: float32 [2, 32768, 767], P('section', 'dp'), may hold values from -6 to 6
- norm_gains: float32 [2, 768], P('section'), may hold values from 0.25 to 1.75
- first_proj: bfloat16 [2, 768, 3072], P('section', None, 'dp'), may hold values from -0.3125 to 0.3125
- down_proj: bfloat16 [768, 3072], P(None, ('section', 'dp')), may hold values from -0.109375 to 0.109375
- doc_lengths: int32 [64, 4], P('dp'), may hold values from 1 to 256, 512 in all within a row
- pad_mask: int32 [32768], P('dp'), may hold values 0 or 1
Outputs:
- layer_out: float32 [2, 32768, 767], P('section', 'dp')
- gain_grad: float32 [2, 768], P('section', 'dp')
- first_grad: float32 [2, 768, 3072], P('section', None, 'dp')
- down_grad: float32 [768, 3072], P(None, ('section', 'dp'))
Inputs may be any that keep to these rules, and one draw needn't show every extreme that they name: `doc_lengths`: each row sums to 512; one sequence of every row has exactly 256 tokens.
All inputs are finite; a program needn't handle non-finite values. No bound on the sum of `pad_mask` on one device may be relied on, other than what follows from the above.
Results may differ from a plain program's by a relative error of at most 0.013.
The roundings to bfloat16 on the way count: a program that leaves them out, or rounds other values in their place, can miss the bound.
Values may be sent and summed in bfloat16 or wider, within the bound.
A program may use at most 384 MiB of HBM per device.

v0:
```python
from functools import partial

import jax
import jax.numpy as jnp
from jax import lax
from jax.sharding import PartitionSpec as P

HEADS = 12
HEAD_DIM = 64
FF = 3072
D = 768
SLOTS = 512
MB = 4


epsilon = 1e-05
masked_score = -1e30


def from_behind(block, axis, distance):
    devices = range(lax.axis_size(axis))
    route = [(i - distance, i) for i in devices if i - distance in devices]
    return lax.ppermute(block, axis, route)


def partner(value, axis, bit):
    return lax.ppermute(value, axis, [(i, i ^ 1 << bit) for i in range(lax.axis_size(axis))])


def expand(stream):
    return jnp.concatenate([stream, -jnp.sum(stream, axis=-1, keepdims=True)], axis=-1)


def shrink(branch):
    return (branch - jnp.mean(branch, axis=-1, keepdims=True))[:, :-1]


def shrink_back(gradient):
    row_total = jnp.sum(gradient, axis=-1, keepdims=True) / (gradient.shape[-1] + 1)
    return jnp.concatenate([gradient - row_total, -row_total], axis=-1)


def inner_rows(left, right):
    return lax.dot_general(
        left, right, (((0,), (0,)), ((), ())), preferred_element_type=jnp.float32
    )


def outer_cols(left, right):
    return lax.dot_general(
        left, right, (((1,), (1,)), ((), ())), preferred_element_type=jnp.float32
    )


def norm_forward(expanded, gain):
    inverse = lax.rsqrt(jnp.mean(expanded * expanded, axis=-1, keepdims=True) + epsilon)
    return (inverse, (expanded * inverse * gain).astype(jnp.bfloat16))


def norm_backward(expanded, inverse, gain, gradient):
    scaled = gain * gradient
    input_grad = inverse * scaled - expanded * (inverse * inverse * inverse) * jnp.mean(
        expanded * scaled, axis=-1, keepdims=True
    )
    return (input_grad, jnp.sum(gradient * expanded * inverse, axis=0))


def expand_back(input_grad, gradient):
    return gradient + input_grad[:, :-1] - input_grad[:, -1:]


def visibility(lengths, token_marks, first_row, block_rows):
    doc_ends = jnp.cumsum(lengths)
    key_pos = lax.iota(jnp.int32, SLOTS)
    queries = first_row + lax.iota(jnp.int32, block_rows)
    key_doc = jnp.sum((key_pos[:, None] >= doc_ends[None, :]).astype(jnp.int32), axis=1)
    query_doc = jnp.sum((queries[:, None] >= doc_ends[None, :]).astype(jnp.int32), axis=1)
    same_doc = query_doc[:, None] == key_doc[None, :]
    causal = key_pos[None, :] <= queries[:, None]
    key_live = (token_marks[None, :] == 1) | (key_pos[None, :] == queries[:, None])
    return same_doc & causal & key_live


def split_heads(projected):
    query_heads = projected[:, :D].reshape(SLOTS, HEADS, HEAD_DIM)
    key_heads = projected[:, D : 2 * D].reshape(SLOTS, HEADS, HEAD_DIM)
    value_heads = projected[:, 2 * D :].reshape(SLOTS, HEADS, HEAD_DIM)
    return (query_heads, key_heads, value_heads)


def block_scores(query_block, key_heads, lengths, token_marks, first_row, block_rows):
    visible = visibility(lengths, token_marks, first_row, block_rows)
    scores = jnp.einsum(
        "qhd,khd->hqk", query_block, key_heads, preferred_element_type=jnp.float32
    ) * HEAD_DIM ** (-0.5)
    return jnp.where(visible[None], scores, masked_score)


def attention_forward(stream, gain, full_weight, lengths, token_marks):
    block_rows = min(512, SLOTS)
    blocks = SLOTS // block_rows
    expanded = expand(stream)
    inverse, normed = norm_forward(expanded, gain)
    projected = jnp.dot(normed, full_weight[:, : 3 * D], preferred_element_type=jnp.float32).astype(
        jnp.bfloat16
    )
    query_heads, key_heads, value_heads = split_heads(projected)

    def forward_block(block_index):
        first_row = block_index * block_rows
        scores = block_scores(query_heads, key_heads, lengths, token_marks, first_row, block_rows)
        highest = jnp.max(scores, axis=-1, keepdims=True)
        log_total = highest + jnp.log(jnp.sum(jnp.exp(scores - highest), axis=-1, keepdims=True))
        rounded = jnp.exp(scores - log_total).astype(jnp.bfloat16)
        attended = jnp.einsum(
            "hqk,khd->qhd", rounded, value_heads, preferred_element_type=jnp.float32
        )
        return (attended.astype(jnp.bfloat16), log_total[..., 0])

    attended, log_total = lax.map(forward_block, lax.iota(jnp.int32, blocks))
    attended = attended.reshape(SLOTS, D)
    branch = jnp.dot(attended, full_weight[:, 3 * D :], preferred_element_type=jnp.float32)
    return (stream + shrink(branch), (expanded, inverse, normed, projected, attended, log_total))


def attention_backward(gradient, kept_state, gain, full_weight, lengths, token_marks):
    expanded, inverse, normed, projected, attended, log_total = kept_state
    block_rows = min(512, SLOTS)
    blocks = SLOTS // block_rows
    score_scale = HEAD_DIM ** (-0.5)
    query_heads, key_heads, value_heads = split_heads(projected)
    branch_grad = shrink_back(gradient).astype(jnp.bfloat16)
    out_weight_grad = inner_rows(attended, branch_grad)
    head_grad = (
        outer_cols(branch_grad, full_weight[:, 3 * D :])
        .astype(jnp.bfloat16)
        .reshape(SLOTS, HEADS, HEAD_DIM)
    )

    def backward_block(running, block_index):
        key_grad, value_grad = running
        first_row = block_index * block_rows
        scores = block_scores(query_heads, key_heads, lengths, token_marks, first_row, block_rows)
        probs_full = jnp.exp(scores - log_total[block_index][..., None])
        rounded = probs_full.astype(jnp.bfloat16)
        probs_grad = jnp.einsum(
            "qhd,khd->hqk", head_grad, value_heads, preferred_element_type=jnp.float32
        )
        score_grad = (
            probs_full * (probs_grad - jnp.sum(probs_full * probs_grad, axis=-1, keepdims=True))
        ).astype(jnp.bfloat16)
        query_grad = (
            jnp.einsum("hqk,khd->qhd", score_grad, key_heads, preferred_element_type=jnp.float32)
            * score_scale
        )
        key_grad = (
            key_grad
            + jnp.einsum(
                "hqk,qhd->khd", score_grad, query_heads, preferred_element_type=jnp.float32
            )
            * score_scale
        )
        value_grad = value_grad + jnp.einsum(
            "hqk,qhd->khd", rounded, head_grad, preferred_element_type=jnp.float32
        )
        return ((key_grad, value_grad), query_grad)

    zero_heads = jnp.zeros((SLOTS, HEADS, HEAD_DIM), jnp.float32)
    (key_grad, value_grad), query_grad = lax.scan(
        backward_block, (zero_heads, zero_heads), lax.iota(jnp.int32, blocks)
    )
    projected_grad = jnp.concatenate(
        [query_grad.reshape(SLOTS, D), key_grad.reshape(SLOTS, D), value_grad.reshape(SLOTS, D)],
        axis=1,
    ).astype(jnp.bfloat16)
    in_weight_grad = inner_rows(normed, projected_grad)
    normed_grad = outer_cols(projected_grad, full_weight[:, : 3 * D])
    input_grad, gain_grad = norm_backward(expanded, inverse, gain, normed_grad)
    return (
        expand_back(input_grad, gradient),
        jnp.concatenate([in_weight_grad, out_weight_grad], axis=1),
        gain_grad,
    )


def mixer_pass(middle_stream, gradient, gain, full_weight, down_full):
    expanded = expand(middle_stream)
    inverse, normed = norm_forward(expanded, gain)
    pre_act = jnp.dot(normed, full_weight, preferred_element_type=jnp.float32)
    activated_full, gelu_pullback = jax.vjp(partial(jax.nn.gelu, approximate=True), pre_act)
    activated = activated_full.astype(jnp.bfloat16)
    branch = outer_cols(activated, down_full)
    result = middle_stream + shrink(branch)
    branch_grad = shrink_back(gradient).astype(jnp.bfloat16)
    down_term = inner_rows(branch_grad, activated)
    gelu_grad = jnp.dot(branch_grad, down_full, preferred_element_type=jnp.float32)
    pre_grad = gelu_pullback(gelu_grad)[0].astype(jnp.bfloat16)
    up_term = inner_rows(normed, pre_grad)
    normed_grad = outer_cols(pre_grad, full_weight)
    input_grad, gain_grad = norm_backward(expanded, inverse, gain, normed_grad)
    return (result, expand_back(input_grad, gradient), up_term, down_term, gain_grad)


def shards(stream_pair, norm_gains, first_proj, down_proj, doc_lengths, pad_mask):
    on_attention = lax.axis_index("section") == 0
    own_rows = stream_pair[0]
    own_gain = norm_gains[0]
    own_local = first_proj[0]
    token_marks = pad_mask.reshape(MB, SLOTS)
    width = own_rows.shape[1]
    block_rows = min(512, SLOTS)
    blocks = SLOTS // block_rows
    empty_rows = jnp.zeros((SLOTS, width), jnp.float32)
    empty_first = jnp.zeros((D, FF), jnp.float32)
    empty_gain = jnp.zeros((D,), jnp.float32)
    empty_state = (
        jnp.zeros((SLOTS, D), jnp.float32),
        jnp.zeros((SLOTS, 1), jnp.float32),
        jnp.zeros((SLOTS, D), jnp.bfloat16),
        jnp.zeros((SLOTS, 3 * D), jnp.bfloat16),
        jnp.zeros((SLOTS, D), jnp.bfloat16),
        jnp.zeros((blocks, HEADS, block_rows), jnp.float32),
    )

    def buffer_rows(micro):
        return own_rows[micro * SLOTS : (micro + 1) * SLOTS]

    incoming = empty_rows
    kept_states = {}
    produced = []
    totals = None
    for step_index in range(MB + 2):
        fetch_full_weight = lax.all_gather(own_local, "dp", axis=1, tiled=True)
        half_down = lax.all_gather(down_proj, "dp", axis=1, tiled=True)
        other_half = from_behind(half_down, "section", 1)
        full_weight = fetch_full_weight
        down_full = jnp.concatenate([other_half, half_down], axis=1)
        forward_mb = step_index if step_index < MB else -1
        backward_mb = step_index - 2
        mixer_mb = step_index - 1 if step_index <= MB else -1

        def attention_side():
            row_block, first_term, gain_term = (empty_rows, empty_first, empty_gain)
            outgoing, kept_state = (empty_rows, empty_state)
            if backward_mb >= 0:
                row_block, first_term, gain_term = attention_backward(
                    incoming,
                    kept_states[backward_mb],
                    own_gain,
                    full_weight,
                    doc_lengths[backward_mb],
                    token_marks[backward_mb],
                )
            if forward_mb >= 0:
                outgoing, kept_state = attention_forward(
                    buffer_rows(forward_mb),
                    own_gain,
                    full_weight,
                    doc_lengths[forward_mb],
                    token_marks[forward_mb],
                )
            return (outgoing, row_block, first_term, empty_first, gain_term, kept_state)

        def mixer_side():
            if mixer_mb >= 0:
                gradient = buffer_rows(mixer_mb) * token_marks[mixer_mb][:, None].astype(
                    jnp.float32
                )
                result, stream_grad, up_term, down_term, gain_term = mixer_pass(
                    incoming, gradient, own_gain, full_weight, down_full
                )
                return (stream_grad, result, up_term, down_term, gain_term, empty_state)
            return (empty_rows, empty_rows, empty_first, empty_first, empty_gain, empty_state)

        outgoing, row_block, first_term, down_term, gain_term, kept_state = lax.cond(
            on_attention, attention_side, mixer_side
        )
        if forward_mb >= 0:
            kept_states[forward_mb] = kept_state
        produced.append(row_block)
        if step_index <= MB:
            incoming = partner(outgoing, "section", 0)
        if step_index >= 1:
            lower_half = from_behind(
                down_term[:, : FF // 2].astype(jnp.bfloat16), "section", -1
            ).astype(jnp.float32)
            own_half = jnp.where(on_attention, lower_half, down_term[:, FF // 2 :])
            shares = (
                lax.psum_scatter(first_term, "dp", scatter_dimension=1, tiled=True),
                lax.psum_scatter(own_half, "dp", scatter_dimension=1, tiled=True),
                lax.psum_scatter(gain_term, "dp", scatter_dimension=0, tiled=True),
            )
            totals = shares if totals is None else jax.tree.map(jnp.add, totals, shares)
    finished = [
        jnp.where(on_attention, produced[micro + 2], produced[micro + 1]) for micro in range(MB)
    ]
    layer_out = jnp.concatenate(finished, axis=0)[None]
    first_share, down_share, gain_share = totals
    return (layer_out, gain_share[None], first_share[None], down_share)


def solution(mesh):
    placed = (
        P("section", "dp", None),
        P("section", None),
        P("section", None, "dp"),
        P(None, ("section", "dp")),
        P("dp", None),
        P("dp"),
    )
    return jax.shard_map(
        shards,
        mesh=mesh,
        in_specs=placed,
        out_specs=(
            P("section", "dp", None),
            P("section", "dp"),
            P("section", None, "dp"),
            P(None, ("section", "dp")),
        ),
        check_vma=False,
    )
```

profile of v0, /device:TPU:1, one launch (start us, length us, event | category | flops | bytes accessed | tf_op | source)
XLA Modules:
  0.0 970.0 jit_solution(11935266347089570181)
XLA Ops:
  8.7 65.9 %all-gather.4.cloned.1.call-done = bf16[768,1536]{0,1:T(8,128)(2,1)} async-done(((bf16[768,96]{0,1:T(8,128)(2,1)}), bf16[768,1536]{0,1:T(8,128)(2,1)}) %all-gather.4.cloned.1.call-update) | async-done | bytes 2359312 | tf_op jit(solution)/shard_map/all_gather | solution.py:234
  76.6 16.1 %copy.320 = f32[1,2048,767]{2,1,0:T(8,128)} copy(f32[1,2048,767]{1,0,2:T(1,128)} %param.18) | data formatting | bytes 12566528 | tf_op args[0]
  92.7 63.8 %all-gather.6.cloned.1.call-done = bf16[1,768,3072]{1,2,0:T(8,128)(2,1)} async-done(((bf16[1,768,192]{1,2,0:T(8,128)(2,1)}), bf16[1,768,3072]{1,2,0:T(8,128)(2,1)}) %all-gather.6.cloned.1.call-update) | async-done | bytes 4718608 | tf_op jit(solution)/shard_map/all_gather | solution.py:233
  161.9 30.8 %collective-permute-start = (f32[512,767]{1,0:T(8,128)}, f32[512,767]{1,0:T(8,128)S(1)}, u32[]{:S(2)}, u32[]{:S(2)}) collective-permute-start(f32[512,767]{1,0:T(8,128)} %get-tuple-element.696), channel_id=1, source_target_pairs={{0,16},{16,0},{1,17},{17,1},{2,18},{18,2},{3,19},{19,3},{4,20},{20... | collective-permute-start | bytes 4712456 | tf_op jit(solution)/shard_map/ppermute | solution.py:27
  197.5 54.1 %conditional.7 = (f32[512,767]{1,0:T(8,128)}, f32[768]{0:T(1024)S(1)}, f32[512,768]{1,0:T(8,128)S(1)}, f32[512,1]{1,0:T(8,128)}, bf16[512,768]{1,0:T(8,128)(2,1)...) conditional(s32[]{:T(128)} %convert_element_type.329, ...), branch_computations={%region_9.16_spmd, %region_16.24_spmd} | conditional | flops 14572582912 | bytes 188841280 | solution.py:275
  206.7 8.5 fusion.200
  260.0 77.4 %conditional.8 = (f32[512,767]{1,0:T(8,128)}, f32[768,3072]{0,1:T(8,128)}, f32[512,768]{1,0:T(8,128)}, f32[512,1]{0,1:T(1,128)S(1)}, bf16[512,768]{1,0:T(8,128)(...) conditional(s32[]{:T(128)} %convert_element_type.329, ...), branch_computations={%region_24.30_spmd, %region_30.43_spmd} | conditional | flops 14569830400 | bytes 338781184 | solution.py:275
  271.6 8.5 fusion.209
  299.4 10.4 %fusion.53 = f32[768,3072]{0,1:T(8,128)} fusion(bf16[512,1]{1,0:T(8,128)(2,1)S(1)} %copy-done.92, bf16[512,767]{1,0:T(8,128)(2,1)} %copy-done.78, f32[512,3072]{1,0:T(8,128)} %copy-done.125), kind=kOutput, calls=%fused_computation.124 | convolution fusion | flops 2431647744 | bytes 16515072 | tf_op jit(solution)/shard_map/cond | solution.py:275
  338.6 48.4 %collective-permute-start.3 = (f32[512,767]{1,0:T(8,128)}, f32[512,767]{1,0:T(8,128)S(1)}, u32[]{:S(2)}, u32[]{:S(2)}) collective-permute-start(f32[512,767]{1,0:T(8,128)} %get-tuple-element.706), channel_id=1, source_target_pairs={{0,16},{16,0},{1,17},{17,1},{2,18},{18,2},{3,19},{19,3},{4,20},{20... | collective-permute-start | bytes 4712456 | tf_op jit(solution)/shard_map/ppermute | solution.py:27
  390.2 81.8 %conditional.9 = (f32[512,767]{1,0:T(8,128)}, f32[768,3072]{0,1:T(8,128)}, f32[512,768]{1,0:T(8,128)}, f32[512,1]{0,1:T(1,128)}, bf16[512,768]{1,0:T(8,128)(2,1)...) conditional(s32[]{:T(128)} %convert_element_type.329, ...), branch_computations={%region_43.0_spmd, %region_49.62_spmd} | conditional | flops 14569830400 | bytes 351351840 | solution.py:275
  404.3 8.5 fusion.214
  431.9 10.4 %fusion.103 = f32[768,3072]{0,1:T(8,128)} fusion(bf16[512,1]{1,0:T(8,128)(2,1)S(1)} %copy-done.93, bf16[512,767]{1,0:T(8,128)(2,1)} %copy-done.79, f32[512,3072]{1,0:T(8,128)} %copy-done.126), kind=kOutput, calls=%fused_computation.234 | convolution fusion | flops 2431647744 | bytes 16515072 | tf_op jit(solution)/shard_map/cond | solution.py:275
  473.2 45.2 %collective-permute-start.4 = (f32[512,767]{1,0:T(8,128)}, f32[512,767]{1,0:T(8,128)S(1)}, u32[]{:S(2)}, u32[]{:S(2)}) collective-permute-start(f32[512,767]{1,0:T(8,128)} %get-tuple-element.714), channel_id=1, source_target_pairs={{0,16},{16,0},{1,17},{17,1},{2,18},{18,2},{3,19},{19,3},{4,20},{20... | collective-permute-start | bytes 4712456 | tf_op jit(solution)/shard_map/ppermute | solution.py:27
  543.4 71.7 %conditional.10 = (f32[512,767]{1,0:T(8,128)}, f32[768,3072]{0,1:T(8,128)}, f32[]{:T(128)}, f32[512,768]{1,0:T(8,128)S(1)}, f32[512,768]{1,0:T(8,128)}, /*index=...) conditional(s32[]{:T(128)} %convert_element_type.329, ...), branch_computations={%region_62.68_spmd, %region_68.74_spmd} | conditional | flops 14569830400 | bytes 257703552 | solution.py:275
  553.0 8.5 fusion.219
  584.9 10.1 %fusion.153 = f32[768,3072]{0,1:T(8,128)} fusion(bf16[512,1]{1,0:T(8,128)(2,1)S(1)} %neg.240, bf16[512,767]{1,0:T(8,128)(2,1)S(1)} %copy-done.81, f32[512,3072]{1,0:T(8,128)} %copy-done.127), kind=kOutput, calls=%fused_computation.344 | convolution fusion | flops 2431647744 | bytes 16515072 | tf_op jit(solution)/shard_map/cond | solution.py:275
  618.2 17.9 %collective-permute-start.9 = (bf16[768,1536]{0,1:T(8,128)(2,1)S(1)}, bf16[768,1536]{0,1:T(8,128)(2,1)S(1)}, u32[]{:S(2)}, u32[]{:S(2)}) collective-permute-start(bf16[768,1536]{0,1:T(8,128)(2,1)S(1)} %slice.584), channel_id=1, source_target_pairs={{16,0},{17,1},{18,2},{19,3},{20,4},{21,5},{22,6},{23,7},{24,8},{25... | collective-permute-start | bytes 7077896 | tf_op jit(solution)/shard_map/ppermute | solution.py:23
  640.2 11.5 %add_add_fusion.1 = f32[768,1536]{0,1:T(8,128)} fusion(bf16[768,1536]{0,1:T(8,128)(2,1)} %collective-permute-done.10, f32[768,1536]{0,1:T(8,128)} %get-tuple-element.1233, bf16[768,1536]{0,1:T(8,128)(2,1)S(1)} %collective-permute-done.9, f32[768,1536]{0,1:T(8,128)} %get-tuple-element.1230, bf16[768,1536]{0,1:T(8,128)(2,1)} %collective-permute-done.8, ...), kind=kLoop, calls=%fused_computation.452 | loop fusion | flops 16515072 | bytes 35389440 | tf_op jit(solution)/shard_map/add | solution.py:293
  655.4 9.8 %conditional.11 = (f32[768,3072]{0,1:T(8,128)}, f32[768]{0:T(1024)}, f32[512,767]{0,1:T(8,128)}) conditional(s32[]{:T(128)} %convert_element_type.329, () %tuple.102, (f32[512,1]{0,1:T(1,128)S(1)}, f32[1,768]{1,0:T(1,128)S(1)}, s32[4,4]{1,0:T(4,128)}, s32[4,512]{1,0:T(4,128)S(1)}, bf16[512,2304]{1,0:T(8,128)(2,1)}, ...), branch_computations={%region_74.75_spmd, %region_75.82_spmd} | conditional | flops 6922172928 | bytes 237249056 | solution.py:275
  665.2 20.5 %add_add_fusion = f32[768,3072]{0,1:T(8,128)} fusion(f32[768,3072]{0,1:T(8,128)} %get-tuple-element.748, f32[768,3072]{0,1:T(8,128)} %get-tuple-element.747, f32[768,3072]{0,1:T(8,128)} %get-tuple-element.746, f32[768,3072]{0,1:T(8,128)} %copy-done.16, f32[768,3072]{0,1:T(8,128)} %get-tuple-element.745), kind=kLoop, calls=%fused_computation.446 | loop fusion | flops 9437184 | bytes 56623104 | tf_op jit(solution)/shard_map/add | solution.py:293
  704.8 32.5 %all-reduce = f32[768]{0:T(1024)S(1)} all-reduce(f32[768]{0:T(1024)S(1)} %add_add_fusion.2), channel_id=15, replica_groups=mesh['section'=2,'dp'=16] {'dp'}, use_global_device_ids=true, to_apply=%region_82.83.clone | all-reduce | flops 768 | bytes 6144
  737.9 47.4 %reduce-scatter.5.cloned.1.call-done = f32[768,96]{0,1:T(8,128)} async-done(((f32[768,1536]{0,1:T(8,128)}), f32[768,96]{0,1:T(8,128)}) %reduce-scatter.5.cloned.1.call-update) | async-done | bytes 294928 | tf_op jit(solution)/shard_map/reduce_scatter | solution.py:290
  785.2 177.7 %reduce-scatter.3.cloned.1.call-done = f32[768,192]{0,1:T(8,128)} async-done(((f32[768,3072]{0,1:T(8,128)}), f32[768,192]{0,1:T(8,128)}) %reduce-scatter.3.cloned.1.call-update) | async-done | bytes 589840 | tf_op jit(solution)/shard_map/reduce_scatter | solution.py:289
  (267 shorter events, 270.9 us)
Async XLA Ops:
  7.2 67.4 %all-gather.4.cloned.1.call-start = ((), (), s32[]{:S(2)}) async-start(), calls=%async_computation.2 | async-start | bytes 2506752 | tf_op jit(solution)/shard_map/all_gather | solution.py:234
  7.9 148.6 %all-gather.6.cloned.1.call-start = ((), (), s32[]{:S(2)}) async-start(), calls=%async_computation.3 | async-start | bytes 5013504 | tf_op jit(solution)/shard_map/all_gather | solution.py:233
  8.6 776.6 %reduce-scatter.5.cloned.1.call-start = ((), (), s32[]{:S(2)}) async-start(), calls=%async_computation.5 | async-start | bytes 5013504 | tf_op jit(solution)/shard_map/reduce_scatter | solution.py:290
  74.6 118.1 %collective-permute-start.1 = (bf16[768,1536]{0,1:T(8,128)(2,1)}, bf16[768,1536]{0,1:T(8,128)(2,1)}, u32[]{:S(2)}, u32[]{:S(2)}) collective-permute-start(bf16[768,1536]{0,1:T(8,128)(2,1)} %all-gather.4.cloned.1.call-done), channel_id=1, source_target_pairs={{0,16},{1,17},{2,18},{3,19},{4,20},{5,21},{6,22},{7,23},{8,24},{9,... | collective-permute-start | bytes 7077896 | tf_op jit(solution)/shard_map/ppermute | solution.py:23
  76.6 79.9 %copy-start.83 = (f32[1,768]{1,0:T(1,128)S(1)}, f32[1,768]{1,0:T(1,128)}, u32[]{:S(2)}) copy-start(f32[1,768]{1,0:T(1,128)} %param.19) | copy-start | bytes 9220
  76.6 79.9 %copy-start.115 = (s32[4,4]{1,0:T(4,128)S(1)}, s32[4,4]{1,0:T(4,128)}, u32[]{:S(2)}) copy-start(s32[4,4]{1,0:T(4,128)} %param.22) | copy-start | bytes 196
  161.9 35.6 %copy-start.11 = (f32[512,768]{1,0:T(8,128)}, f32[512,768]{1,0:T(8,128)S(1)}, u32[]{:S(2)}) copy-start(f32[512,768]{1,0:T(8,128)S(1)} %get-tuple-element.701) | copy-start | bytes 4718596
  161.9 34.0 %copy-start.75 = (bf16[768,1536]{0,1:T(8,128)(2,1)S(1)}, bf16[768,1536]{0,1:T(8,128)(2,1)}, u32[]{:S(2)}) copy-start(bf16[768,1536]{0,1:T(8,128)(2,1)} %all-gather.4.cloned.1.call-done) | copy-start | bytes 7077892
  161.9 35.6 %collective-permute-start = (f32[512,767]{1,0:T(8,128)}, f32[512,767]{1,0:T(8,128)S(1)}, u32[]{:S(2)}, u32[]{:S(2)}) collective-permute-start(f32[512,767]{1,0:T(8,128)} %get-tuple-element.696), channel_id=1, source_target_pairs={{0,16},{16,0},{1,17},{17,1},{2,18},{18,2},{3,19},{19,3},{4,20},{20... | collective-permute-start | bytes 4712456 | tf_op jit(solution)/shard_map/ppermute | solution.py:27
  251.7 3.7 collective-permute-start.2
  265.4 26.6 %copy-start.13 = (f32[512,768]{1,0:T(8,128)}, f32[512,768]{1,0:T(8,128)S(1)}, u32[]{:S(2)}) copy-start(f32[512,768]{1,0:T(8,128)S(1)} %get-tuple-element.1432) | copy-start | bytes 4718596 | tf_op jit(solution)/shard_map/cond
  338.6 51.6 %copy-start.19 = (f32[512,768]{1,0:T(8,128)}, f32[512,768]{1,0:T(8,128)S(1)}, u32[]{:S(2)}) copy-start(f32[512,768]{1,0:T(8,128)S(1)} %get-tuple-element.733) | copy-start | bytes 4718596
  338.6 51.6 %collective-permute-start.3 = (f32[512,767]{1,0:T(8,128)}, f32[512,767]{1,0:T(8,128)S(1)}, u32[]{:S(2)}, u32[]{:S(2)}) collective-permute-start(f32[512,767]{1,0:T(8,128)} %get-tuple-element.706), channel_id=1, source_target_pairs={{0,16},{16,0},{1,17},{17,1},{2,18},{18,2},{3,19},{19,3},{4,20},{20... | collective-permute-start | bytes 4712456 | tf_op jit(solution)/shard_map/ppermute | solution.py:27
  396.2 51.2 %copy-start.7 = (f32[512,768]{1,0:T(8,128)}, f32[512,768]{1,0:T(8,128)S(1)}, u32[]{:S(2)}) copy-start(f32[512,768]{1,0:T(8,128)S(1)} %get-tuple-element.1462) | copy-start | bytes 4718596 | tf_op jit(solution)/shard_map/cond
  473.2 70.2 %collective-permute-start.4 = (f32[512,767]{1,0:T(8,128)}, f32[512,767]{1,0:T(8,128)S(1)}, u32[]{:S(2)}, u32[]{:S(2)}) collective-permute-start(f32[512,767]{1,0:T(8,128)} %get-tuple-element.714), channel_id=1, source_target_pairs={{0,16},{16,0},{1,17},{17,1},{2,18},{18,2},{3,19},{19,3},{4,20},{20... | collective-permute-start | bytes 4712456 | tf_op jit(solution)/shard_map/ppermute | solution.py:27
  520.0 116.1 %collective-permute-start.10 = (bf16[768,1536]{0,1:T(8,128)(2,1)}, bf16[768,1536]{0,1:T(8,128)(2,1)}, u32[]{:S(2)}, u32[]{:S(2)}) collective-permute-start(bf16[768,1536]{0,1:T(8,128)(2,1)} %broadcast.1036), channel_id=1, source_target_pairs={{16,0},{17,1},{18,2},{19,3},{20,4},{21,5},{22,6},{23,7},{24,8},{25... | collective-permute-start | bytes 7077896 | tf_op jit(solution)/shard_map/ppermute | solution.py:23
  527.3 108.9 %collective-permute-start.6 = (bf16[768,1536]{0,1:T(8,128)(2,1)}, bf16[768,1536]{0,1:T(8,128)(2,1)}, u32[]{:S(2)}, u32[]{:S(2)}) collective-permute-start(bf16[768,1536]{0,1:T(8,128)(2,1)} %slice.587), channel_id=1, source_target_pairs={{16,0},{17,1},{18,2},{19,3},{20,4},{21,5},{22,6},{23,7},{24,8},{25... | collective-permute-start | bytes 7077896 | tf_op jit(solution)/shard_map/ppermute | solution.py:23
  534.0 102.2 %collective-permute-start.7 = (bf16[768,1536]{0,1:T(8,128)(2,1)}, bf16[768,1536]{0,1:T(8,128)(2,1)}, u32[]{:S(2)}, u32[]{:S(2)}) collective-permute-start(bf16[768,1536]{0,1:T(8,128)(2,1)} %slice.586), channel_id=1, source_target_pairs={{16,0},{17,1},{18,2},{19,3},{20,4},{21,5},{22,6},{23,7},{24,8},{25... | collective-permute-start | bytes 7077896 | tf_op jit(solution)/shard_map/ppermute | solution.py:23
  540.7 95.5 %collective-permute-start.8 = (bf16[768,1536]{0,1:T(8,128)(2,1)}, bf16[768,1536]{0,1:T(8,128)(2,1)}, u32[]{:S(2)}, u32[]{:S(2)}) collective-permute-start(bf16[768,1536]{0,1:T(8,128)(2,1)} %slice.585), channel_id=1, source_target_pairs={{16,0},{17,1},{18,2},{19,3},{20,4},{21,5},{22,6},{23,7},{24,8},{25... | collective-permute-start | bytes 7077896 | tf_op jit(solution)/shard_map/ppermute | solution.py:23
  615.0 36.6 %copy-start.20 = (f32[512,768]{1,0:T(8,128)}, f32[512,768]{1,0:T(8,128)S(1)}, u32[]{:S(2)}) copy-start(f32[512,768]{1,0:T(8,128)S(1)} %get-tuple-element.741) | copy-start | bytes 4718596
  615.0 25.1 %copy-start.18 = (f32[768,1536]{0,1:T(8,128)S(1)}, f32[768,1536]{0,1:T(8,128)}, u32[]{:S(2)}) copy-start(f32[768,1536]{0,1:T(8,128)} %copy-done.17) | copy-start | bytes 14155780
  618.2 21.9 %collective-permute-start.9 = (bf16[768,1536]{0,1:T(8,128)(2,1)S(1)}, bf16[768,1536]{0,1:T(8,128)(2,1)S(1)}, u32[]{:S(2)}, u32[]{:S(2)}) collective-permute-start(bf16[768,1536]{0,1:T(8,128)(2,1)S(1)} %slice.584), channel_id=1, source_target_pairs={{16,0},{17,1},{18,2},{19,3},{20,4},{21,5},{22,6},{23,7},{24,8},{25... | collective-permute-start | bytes 7077896 | tf_op jit(solution)/shard_map/ppermute | solution.py:23
  651.7 311.3 %reduce-scatter.3.cloned.1.call-start = ((), (), s32[]{:S(2)}) async-start(), calls=%async_computation.4 | async-start | bytes 10027008 | tf_op jit(solution)/shard_map/reduce_scatter | solution.py:289
  651.7 3.7 collective-permute-start.5
  (42 other events, 271.3 us)
Sparse Core Ops, SparseCore 0:
  10.8 63.7 all-gather.3
  77.4 79.0 all-gather.5
  651.8 133.3 reduce-scatter.4
  792.3 170.6 reduce-scatter.2
where the time goes:
time: 985 us; the launch traced here: 970 us
  waiting for transfers between devices  371 us (38%)
  matrix products  157 us (16%)
  starting transfers between devices  155 us (16%)
  local copies, waits for them, and re-layouts  113 us (11%)
  other arithmetic  79.5 us (8%)
  loops' own time  46.9 us (5%)
  blocking collectives  32.5 us (3%)
  between operations  15.2 us (2%)
    reduce_scatter x1, waiting for transfers between devices, shards(): lax.psum_scatter(first_term, 'dp', scatter_dimension=1, tiled=True)  178 us
    ppermute x5, starting transfers between devices, partner(): lax.ppermute(value, axis, [(i, i ^ 1 << bit) for i in range(lax.axis_size...  125 us
    all_gather x1, waiting for transfers between devices, shards(): half_down = lax.all_gather(down_proj, 'dp', axis=1, tiled=True)  65.9 us
    all_gather x1, waiting for transfers between devices, shards(): fetch_full_weight = lax.all_gather(own_local, 'dp', axis=1, tiled=True)  63.8 us
    dot_general x8, matrix products, outer_cols(): lax.dot_general(left, right, (((1,), (1,)), ((), ())), preferred_element_...  50.6 us
    reduce_scatter x1, waiting for transfers between devices, shards(): lax.psum_scatter(own_half, 'dp', scatter_dimension=1, tiled=True)  47.4 us
    another operation x6, loops' own time, shards(): lax.cond(on_attention, attention_side, mixer_side)  46.9 us
    cond x5, matrix products, shards(): lax.cond(on_attention, attention_side, mixer_side)  40.8 us
  transfers between devices with their start and end apart: 15, of which 8 were waited for; matrix products, arithmetic and copies ran while one was open for 16% of the time, Pallas kernels for 0%

commit v1 on v0

v1 whole, which is shorter than its diff:
```python
import functools
import jax, jax.numpy as jnp
from jax import lax
from jax.experimental import pallas as pl
from jax.experimental.pallas import tpu as pltpu
from jax.sharding import PartitionSpec as P

HEADS, HEAD_DIM, FF, D, SLOTS = 12, 64, 3072, 768, 512
EPS, MASKED = 1e-05, -1e30
f32, bf16 = jnp.float32, jnp.bfloat16
CHUNK = 768

def nn(a, b):
    return lax.dot_general(a, b, (((1,), (0,)), ((), ())), preferred_element_type=f32)
def nt(a, b):
    return lax.dot_general(a, b, (((1,), (1,)), ((), ())), preferred_element_type=f32)
def tn(a, b):
    return lax.dot_general(a, b, (((0,), (0,)), ((), ())), preferred_element_type=f32)

def last_row(shape):
    return lax.broadcasted_iota(jnp.int32, shape, 0) == shape[0] - 1

def expanded(x):
    return jnp.where(last_row(x.shape), -jnp.sum(x, axis=0, keepdims=True), x)

def inv_rms(x):
    return lax.rsqrt(jnp.mean(x * x, axis=0, keepdims=True) + EPS)

def bias_block(ends, live, first_key, keys, first_query, queries):
    shape = (keys, queries)
    kp = lax.broadcasted_iota(jnp.int32, shape, 0) + first_key
    qp = lax.broadcasted_iota(jnp.int32, shape, 1) + first_query
    kd = sum((kp >= e).astype(jnp.int32) for e in ends)
    qd = sum((qp >= e).astype(jnp.int32) for e in ends)
    seen = (kd == qd) & (kp <= qp) & ((live > 0.5) | (kp == qp))
    return jnp.where(seen, 0.0, MASKED)

def attn_fwd(ends_ref, x_ref, g0_ref, g1_ref, mask_ref, w_ref,
             qkv_ref, att_ref, lse_ref, h0_ref, x1_ref, h1_ref, bias_ref):
    T = x_ref.shape[1]
    nb = T // SLOTS
    @pl.loop(0, T // 256)
    def _(t):
        c = pl.ds(pl.multiple_of(t * 256, 256), 256)
        x = expanded(x_ref[:, c])
        h0_ref[:, c] = (x * inv_rms(x) * g0_ref[:, :1]).astype(bf16)
    for b in range(nb):
        ends = [ends_ref[b, j] for j in range(3)]
        marks = jnp.broadcast_to(mask_ref[:1, b * SLOTS:(b + 1) * SLOTS], (128, SLOTS)).T
        for qb in range(2):
            nk = 256 * (qb + 1)
            for q0 in (0, 128):
                bias_ref[b, :nk, qb * 256 + q0: qb * 256 + q0 + 128] = bias_block(ends, marks[:nk], 0, nk, qb * 256 + q0, 128)
    @pl.loop(0, 9)
    def _(m):
        r = pl.ds(pl.multiple_of(m * 256, 256), 256)
        qkv_ref[r, :] = nn(w_ref[r, :], h0_ref[...]).astype(bf16)
    for b in range(nb):
        cols = slice(b * SLOTS, (b + 1) * SLOTS)
        @pl.loop(0, HEADS // 2)
        def _(hp):
            for hh in range(2):
                h = hp * 2 + hh
                off = pl.multiple_of(h * HEAD_DIM, HEAD_DIM)
                q = qkv_ref[pl.ds(off, HEAD_DIM), cols] * bf16(HEAD_DIM ** -0.5)
                k = qkv_ref[pl.ds(off + D, HEAD_DIM), cols].T
                v = qkv_ref[pl.ds(off + 2 * D, HEAD_DIM), cols]
                for qb in range(2):
                    nk, lo = 256 * (qb + 1), qb * 256
                    s = nn(k[:nk], q[:, lo:lo + 256]) + bias_ref[b, :nk, lo:lo + 256]
                    mx = jnp.max(s, axis=0, keepdims=True)
                    p = jnp.exp(s - mx)
                    tot = jnp.sum(p, axis=0, keepdims=True)
                    lse_ref[pl.ds(h, 1), b * SLOTS + lo: b * SLOTS + lo + 256] = mx + jnp.log(tot)
                    low = (p * (1.0 / tot)).astype(bf16)
                    att_ref[pl.ds(off, HEAD_DIM), b * SLOTS + lo: b * SLOTS + lo + 256] = nn(v[:, :nk], low).astype(bf16)
    @pl.loop(0, T // 256)
    def _(t):
        c = pl.ds(pl.multiple_of(t * 256, 256), 256)
        x = expanded(x_ref[:, c])
        a = nn(w_ref[3 * D:, :], att_ref[:, c])
        x1 = expanded(jnp.where(last_row(x.shape), 0.0, x + (a - jnp.mean(a, axis=0, keepdims=True))))
        x1_ref[:, c] = x1
        h1_ref[:, c] = (x1 * inv_rms(x1) * g1_ref[:, :1]).astype(bf16)

C0 = 0.7978845608028654
def gelu_both(u):
    u2 = u * u
    inner = C0 * u * (1.0 + 0.044715 * u2)
    t = jnp.tanh(inner)
    half = 0.5 * (1.0 + t)
    slope = half + 0.5 * u * (1.0 - t * t) * (C0 * (1.0 + 3 * 0.044715 * u2))
    return u * half, slope

def norm_back(x, r, gain, dh):
    e = gain * dh
    dx = r * e - x * (r * r * r) * jnp.mean(x * e, axis=0, keepdims=True)
    return dx, dh * x * r

def lane_fold(v):
    return sum(v[:, i * 128:(i + 1) * 128] for i in range(v.shape[1] // 128))

def ffn(g_ref, g1_ref, mask_ref, x1_ref, h1_ref, w1_ref, wd_ref,
        out1_ref, dy_ref, gw1_ref, gwd_ref, gg_ref, dm_ref, z_ref, du_ref, u_ref, macc, hacc):
    T = g_ref.shape[1]
    nt_ = T // 256
    @pl.loop(0, nt_)
    def _(t):
        c = pl.ds(pl.multiple_of(t * 256, 256), 256)
        g = g_ref[:, c] * mask_ref[:1, c]
        dm_ref[:, c] = (g - jnp.mean(g, axis=0, keepdims=True)).astype(bf16)
    macc[...] = jnp.zeros_like(macc)
    hacc[...] = jnp.zeros_like(hacc)
    @pl.loop(0, FF // CHUNK)
    def _(p):
        base = p * CHUNK
        @pl.loop(0, CHUNK // 256)
        def _(m):
            r = pl.ds(pl.multiple_of(base + m * 256, 256), 256)
            rl = pl.ds(pl.multiple_of(m * 256, 256), 256)
            for n in range(T // 512):
                cs = slice(n * 512, (n + 1) * 512)
                z, slope = gelu_both(nn(w1_ref[r, :], h1_ref[:, cs]))
                z_ref[rl, cs] = z.astype(bf16)
                du_ref[rl, cs] = (nn(wd_ref[r, :], dm_ref[:, cs]) * slope).astype(bf16)
        rows = pl.ds(pl.multiple_of(base, CHUNK), CHUNK)
        @pl.loop(0, 3)
        def _(m):
            o = pl.ds(pl.multiple_of(m * 256, 256), 256)
            macc[o, :] += tn(wd_ref[rows, o], z_ref[...])
            hacc[o, :] += tn(w1_ref[rows, o], du_ref[...])
            r = pl.ds(pl.multiple_of(base + m * 256, 256), 256)
            gw1_ref[r, :] = nt(du_ref[o, :], h1_ref[...]).astype(gw1_ref.dtype)
            gwd_ref[r, :] = nt(z_ref[o, :], dm_ref[...]).astype(gwd_ref.dtype)
    gg_ref[...] = jnp.zeros_like(gg_ref)
    @pl.loop(0, nt_)
    def _(t):
        c = pl.ds(pl.multiple_of(t * 256, 256), 256)
        x1, m = x1_ref[:, c], macc[:, c]
        out1_ref[:, c] = x1 + (m - jnp.mean(m, axis=0, keepdims=True))
        g = g_ref[:, c] * mask_ref[:1, c]
        dx, gg = norm_back(x1, inv_rms(x1), g1_ref[:, :1], hacc[:, c])
        gg_ref[...] += lane_fold(gg)
        dy_ref[:, c] = g + dx - dx[D - 1:, :]

def attn_bwd(ends_ref, x_ref, g0_ref, mask_ref, w_ref, qkv_ref, att_ref, lse_ref, h0_ref, dy_ref,
             out0_ref, gw_ref, gg_ref, da_ref, dat_ref, dqkv_ref, bias_ref):
    T = x_ref.shape[1]
    nb = T // SLOTS
    for b in range(nb):
        ends = [ends_ref[b, j] for j in range(3)]
        marks = jnp.broadcast_to(mask_ref[:1, b * SLOTS:(b + 1) * SLOTS], (128, SLOTS)).T
        for qb in range(2):
            nk = 256 * (qb + 1)
            for q0 in (0, 128):
                bias_ref[b, :nk, qb * 256 + q0: qb * 256 + q0 + 128] = bias_block(ends, marks[:nk], 0, nk, qb * 256 + q0, 128)
    @pl.loop(0, T // 256)
    def _(t):
        c = pl.ds(pl.multiple_of(t * 256, 256), 256)
        dy = dy_ref[:, c]
        da_ref[:, c] = (dy - jnp.mean(dy, axis=0, keepdims=True)).astype(bf16)
    @pl.loop(0, 3)
    def _(m):
        o = pl.ds(pl.multiple_of(m * 256, 256), 256)
        r = pl.ds(pl.multiple_of(3 * D + m * 256, 256), 256)
        gw_ref[r, :] = nt(da_ref[o, :], att_ref[...]).astype(gw_ref.dtype)
        dat_ref[o, :] = tn(w_ref[3 * D:, o], da_ref[...]).astype(bf16)
    for b in range(nb):
        cols = slice(b * SLOTS, (b + 1) * SLOTS)
        @pl.loop(0, HEADS)
        def _(h):
            off = pl.multiple_of(h * HEAD_DIM, HEAD_DIM)
            q = qkv_ref[pl.ds(off, HEAD_DIM), cols] * bf16(HEAD_DIM ** -0.5)
            kt = qkv_ref[pl.ds(off + D, HEAD_DIM), cols]
            k = kt.T
            v = qkv_ref[pl.ds(off + 2 * D, HEAD_DIM), cols].T
            d = dat_ref[pl.ds(off, HEAD_DIM), cols]
            dks, dvs = [], []
            for qb in range(2):
                nk, lo = 256 * (qb + 1), qb * 256
                s = nn(k[:nk], q[:, lo:lo + 256]) + bias_ref[b, :nk, lo:lo + 256]
                p = jnp.exp(s - lse_ref[pl.ds(h, 1), b * SLOTS + lo: b * SLOTS + lo + 256])
                dp = nn(v[:nk], d[:, lo:lo + 256])
                ds = (p * (dp - jnp.sum(p * dp, axis=0, keepdims=True))).astype(bf16)
                low = p.astype(bf16)
                dqkv_ref[pl.ds(off, HEAD_DIM), b * SLOTS + lo: b * SLOTS + lo + 256] = (nn(kt[:, :nk], ds) * HEAD_DIM ** -0.5).astype(bf16)
                dks.append(nt(q[:, lo:lo + 256], ds))
                dvs.append(nt(d[:, lo:lo + 256], low))
            for at, parts in ((D, dks), (2 * D, dvs)):
                dqkv_ref[pl.ds(off + at, HEAD_DIM), b * SLOTS: b * SLOTS + 256] = (parts[0] + parts[1][:, :256]).astype(bf16)
                dqkv_ref[pl.ds(off + at, HEAD_DIM), b * SLOTS + 256: (b + 1) * SLOTS] = parts[1][:, 256:].astype(bf16)
    @pl.loop(0, 9)
    def _(m):
        r = pl.ds(pl.multiple_of(m * 256, 256), 256)
        gw_ref[r, :] = nt(dqkv_ref[r, :], h0_ref[...]).astype(gw_ref.dtype)
    gg_ref[...] = jnp.zeros_like(gg_ref)
    @pl.loop(0, T // 256)
    def _(t):
        c = pl.ds(pl.multiple_of(t * 256, 256), 256)
        x = expanded(x_ref[:, c])
        dh = tn(w_ref[:3 * D, :], dqkv_ref[:, c])
        dx, gg = norm_back(x, inv_rms(x), g0_ref[:, :1], dh)
        gg_ref[...] += lane_fold(gg)
        out0_ref[:, c] = dy_ref[:, c] + dx - dx[D - 1:, :]

V = pl.BlockSpec(memory_space=pltpu.VMEM)
S = pl.BlockSpec(memory_space=pltpu.SMEM)
def sds(*shape, dtype=f32):
    return jax.ShapeDtypeStruct(shape, dtype)
PARAMS = pltpu.CompilerParams(vmem_limit_bytes=60 * 2**20)

def run_attn_fwd(ends, x, g0, g1, mask, w):
    T = x.shape[1]
    return pl.pallas_call(attn_fwd, in_specs=[S] + [V] * 5, out_specs=[V] * 6,
        out_shape=[sds(3 * D, T, dtype=bf16), sds(D, T, dtype=bf16), sds(16, T), sds(D, T, dtype=bf16), sds(D, T), sds(D, T, dtype=bf16)],
        scratch_shapes=[pltpu.VMEM((T // SLOTS, SLOTS, SLOTS), f32)], compiler_params=PARAMS, name="attn_fwd")(ends, x, g0, g1, mask, w)

def run_ffn(g, g1, mask, x1, h1, w1, wd, gdt=bf16):
    T = g.shape[1]
    return pl.pallas_call(ffn, in_specs=[V] * 7, out_specs=[V] * 5,
        out_shape=[sds(D, T), sds(D, T), sds(FF, D, dtype=gdt), sds(FF, D, dtype=gdt), sds(D, 128)],
        scratch_shapes=[pltpu.VMEM((D, T), bf16), pltpu.VMEM((CHUNK, T), bf16), pltpu.VMEM((CHUNK, T), bf16), pltpu.VMEM((8, 128), f32), pltpu.VMEM((D, T), f32), pltpu.VMEM((D, T), f32)],
        compiler_params=PARAMS, name="ffn")(g, g1, mask, x1, h1, w1, wd)

def run_attn_bwd(ends, x, g0, mask, w, qkv, att, lse, h0, dy, gdt=bf16):
    T = x.shape[1]
    return pl.pallas_call(attn_bwd, in_specs=[S] + [V] * 9, out_specs=[V] * 3,
        out_shape=[sds(D, T), sds(FF, D, dtype=gdt), sds(D, 128)],
        scratch_shapes=[pltpu.VMEM((D, T), bf16), pltpu.VMEM((D, T), bf16), pltpu.VMEM((3 * D, T), bf16), pltpu.VMEM((T // SLOTS, SLOTS, SLOTS), f32)],
        compiler_params=PARAMS, name="attn_bwd")(ends, x, g0, mask, w, qkv, att, lse, h0, dy)

MESH = pl.DeviceIdType.MESH
HBM = pl.BlockSpec(memory_space=pl.ANY)


def place():
    s, d = lax.axis_index("section"), lax.axis_index("dp")
    x, y, z = lax.rem(d, 2), lax.rem(d // 2, 2), d // 4
    return s, x, y, z


def neighbours(s, x, y, z):
    at = lambda s, x, y, z: (s, z * 4 + y * 2 + x)
    zs = [at(s, x, y, lax.rem(z + k, 4)) for k in range(1, 4)]
    return at(1 - s, x, y, z), at(s, 1 - x, y, z), at(s, x, 1 - y, z), zs


def greet(devices):
    barrier = pltpu.get_barrier_semaphore()
    for device in devices:
        pl.semaphore_signal(barrier, inc=1, device_id=device, device_id_type=MESH)
    pl.semaphore_wait(barrier, len(devices))


def push(src, dst, send, recv, device):
    copy = pltpu.make_async_remote_copy(
        src_ref=src, dst_ref=dst, send_sem=send, recv_sem=recv, device_id=device, device_id_type=MESH
    )
    copy.start()
    return copy


def gather_kernel(w_ref, wd_ref, s_ref, g_ref, wf, wdf, own_x, own_g, gains, send, recv, local):
    s, x, y, z = place()
    sib, nx, ny, nz = neighbours(s, x, y, z)
    greet([sib, nx, ny, *nz])
    T = own_x.shape[1]
    copies = []
    sets = ((w_ref, wf), (wd_ref, wdf))
    n = 0
    pend = []
    for i, (src, full) in enumerate(sets):
        here = pltpu.make_async_copy(src, full.at[s, z, y, x], local.at[i])
        here.start()
        zc = [push(src, full.at[s, z, y, x], send.at[i, k], recv.at[i, k], nz[k]) for k in range(3)]
        pend.append((here, zc))
    def stream(kind, keep, give, index):
        def go():
            c = pltpu.make_async_copy(s_ref.at[:, pl.ds(index * T, T)], keep, local.at[2])
            c.start()
            r = push(s_ref.at[:, pl.ds((1 - index) * T, T)], keep, send.at[2, 0], recv.at[2, 0], sib)
            c.wait()
            r.wait_send()
        return go
    pl.when(s == 0)(stream(0, own_x, own_x, 0))
    pl.when(s == 1)(stream(1, own_g, own_g, 1))
    gl = pltpu.make_async_copy(g_ref, gains.at[s], local.at[3])
    gl.start()
    gr = push(g_ref, gains.at[s], send.at[2, 1], recv.at[2, 1], sib)
    p2 = []
    for i, (src, full) in enumerate(sets):
        here, zc = pend[i]
        here.wait()
        for c in zc:
            c.wait()
        a = push(full.at[s, :, y, x, 0], full.at[s, :, y, x, 0], send.at[i, 3], recv.at[i, 3], ny)
        b = push(full.at[s, :, y, x, 1], full.at[s, :, y, x, 1], send.at[i, 4], recv.at[i, 4], nx)
        copies.append(push(full.at[s, :, y, x], full.at[s, :, y, x], send.at[i, 5], recv.at[i, 5], sib))
        p2.append((a, b))
    p3 = []
    for i, (src, full) in enumerate(sets):
        a, b = p2[i]
        a.wait()
        c = push(full.at[s, :, :, x, 0], full.at[s, :, :, x, 0], send.at[i, 6], recv.at[i, 6], nx)
        b.wait()
        d = push(full.at[s, :, y, :, 1], full.at[s, :, y, :, 1], send.at[i, 7], recv.at[i, 7], ny)
        copies.append(push(full.at[s, :, 1 - y, x, 0], full.at[s, :, 1 - y, x, 0], send.at[i, 8], recv.at[i, 8], sib))
        copies.append(push(full.at[s, :, y, 1 - x, 1], full.at[s, :, y, 1 - x, 1], send.at[i, 9], recv.at[i, 9], sib))
        p3.append((c, d))
    for i, (src, full) in enumerate(sets):
        c, d = p3[i]
        c.wait()
        copies.append(push(full.at[s, :, :, 1 - x, 0], full.at[s, :, :, 1 - x, 0], send.at[i, 10], recv.at[i, 10], sib))
        d.wait()
        copies.append(push(full.at[s, :, 1 - y, :, 1], full.at[s, :, 1 - y, :, 1], send.at[i, 11], recv.at[i, 11], sib))
    for c in copies:
        c.wait()
    gl.wait()
    gr.wait()
    pl.when(s == 0)(lambda: pltpu.make_async_remote_copy(
        src_ref=own_g, dst_ref=own_g, send_sem=send.at[2, 0], recv_sem=recv.at[2, 0], device_id=sib, device_id_type=MESH).wait_recv())
    pl.when(s == 1)(lambda: pltpu.make_async_remote_copy(
        src_ref=own_x, dst_ref=own_x, send_sem=send.at[2, 0], recv_sem=recv.at[2, 0], device_id=sib, device_id_type=MESH).wait_recv())


def gather(w, wd, stream, gain):
    T = stream.shape[1] // 2
    rows, low = w.shape[0], wd.shape[0]
    shapes = [sds(2, 4, 2, 2, 2, rows // 2, D, dtype=bf16), sds(2, 4, 2, 2, 2, low // 2, D, dtype=bf16),
              sds(D, T), sds(D, T), sds(2, D, 128)]
    wf, wdf, x, g, gains = pl.pallas_call(
        gather_kernel, in_specs=[HBM] * 4, out_specs=[HBM] * 5, out_shape=shapes,
        scratch_shapes=[pltpu.SemaphoreType.DMA((3, 12)), pltpu.SemaphoreType.DMA((3, 12)), pltpu.SemaphoreType.DMA((4,))],
        compiler_params=pltpu.CompilerParams(collective_id=1, has_side_effects=True), name="gather",
    )(w.reshape(2, rows // 2, D), wd.reshape(2, low // 2, D), stream, gain)
    return wf.reshape(2, FF, D), wdf.reshape(FF, D), x, g, gains


def scatter_kernel(gw, gwd, o0, o1, gg, fw, fwd, out, gout,
                   accw, accd, sibw, sibd, l1w, l1d, l2w, l2d, l3w, l3d, gacc, gl, send, recv, local):
    s, x, y, z = place()
    sib, nx, ny, nz = neighbours(s, x, y, z)
    greet([sib, nx, ny, *nz])
    T = o0.shape[1]
    sets = ((gw, fw, accw, sibw, l1w, l2w, l3w), (gwd, fwd, accd, sibd, l1d, l2d, l3d))
    mine = []
    for i, (src, fin, acc, land, *_) in enumerate(sets):
        own = pltpu.make_async_copy(src.at[s], acc, local.at[i])
        own.start()
        mine.append((own, push(src.at[1 - s], land, send.at[i, 0], recv.at[i, 0], sib)))
    own = pltpu.make_async_copy(gg.at[s], gacc, local.at[2])
    own.start()
    gs = push(gg.at[1 - s], gl.at[0], send.at[2, 0], recv.at[2, 0], sib)
    def give(keep, other, index):
        def go():
            c = pltpu.make_async_copy(keep, out.at[:, pl.ds(index * T, T)], local.at[3])
            c.start()
            r = push(other, out.at[:, pl.ds(index * T, T)], send.at[2, 1], recv.at[2, 1], sib)
            c.wait()
            r.wait()
        return go
    def add(acc, index, land):
        acc[index] = (acc[index].astype(f32) + land.astype(f32)).astype(bf16)
    p1 = []
    for i, (src, fin, acc, land, l1, l2, l3) in enumerate(sets):
        own_, rem = mine[i]
        own_.wait()
        rem.wait()
        @pl.loop(0, 4)
        def _(zz):
            for a in range(2):
                for b in range(2):
                    add(acc, (zz, a, b), land[zz, a, b])
        p1.append((push(acc.at[:, :, 1 - x, 0], l1.at[0], send.at[i, 1], recv.at[i, 1], nx),
                   push(acc.at[:, 1 - y, :, 1], l1.at[1], send.at[i, 2], recv.at[i, 2], ny)))
    own.wait()
    gs.wait()
    gacc[...] += gl[0]
    g1 = push(gacc, gl.at[1], send.at[2, 2], recv.at[2, 2], nx)
    pl.when(s == 0)(give(o0, o1, 0))
    pl.when(s == 1)(give(o1, o0, 1))
    g1.wait()
    gacc[...] += gl[1]
    g2 = push(gacc, gl.at[2], send.at[2, 3], recv.at[2, 3], ny)
    g2.wait()
    gacc[...] += gl[2]
    g3 = [push(gacc, gl.at[3 + k], send.at[2, 4 + k], recv.at[2, 4 + k], nz[k]) for k in range(3)]
    p2 = []
    for i, (src, fin, acc, land, l1, l2, l3) in enumerate(sets):
        for c in p1[i]:
            c.wait()
        @pl.loop(0, 4)
        def _(zz):
            for a in range(2):
                add(acc, (zz, a, x, 0), l1[0, zz, a])
                add(acc, (zz, y, a, 1), l1[1, zz, a])
        p2.append((push(acc.at[:, 1 - y, x, 0], l2.at[0], send.at[i, 3], recv.at[i, 3], ny),
                   push(acc.at[:, y, 1 - x, 1], l2.at[1], send.at[i, 4], recv.at[i, 4], nx)))
    p3 = []
    for i, (src, fin, acc, land, l1, l2, l3) in enumerate(sets):
        for c in p2[i]:
            c.wait()
        @pl.loop(0, 4)
        def _(zz):
            add(acc, (zz, y, x, 0), l2[0, zz])
            add(acc, (zz, y, x, 1), l2[1, zz])
        p3.append([push(acc.at[lax.rem(z + k, 4), y, x], l3.at[k - 1], send.at[i, 4 + k], recv.at[i, 4 + k], nz[k - 1]) for k in range(1, 4)])
    for i, (src, fin, acc, land, l1, l2, l3) in enumerate(sets):
        for c in p3[i]:
            c.wait()
        total = acc[z, y, x].astype(f32)
        for k in range(3):
            total += l3[k].astype(f32)
        fin[...] = total
    for c in g3:
        c.wait()
    gout[...] = gacc[...] + gl[3] + gl[4] + gl[5]


def scatter(gw, gwd, out0, out1, gg):
    T = out0.shape[1]
    rows, low = FF // 16, FF // 32
    bulk = lambda r: [pltpu.VMEM((4, 2, 2, 2, r // 2, D), bf16)]
    scratch = []
    for shape in ((4, 2, 2, 2), (4, 2, 2, 2), (2, 4, 2), (2, 4), (3, 2)):
        for r in (rows, low):
            scratch.append(pltpu.VMEM((*shape, r // 2, D), bf16))
    scratch += [pltpu.VMEM((8, D), f32), pltpu.VMEM((6, 8, D), f32)]
    scratch += [pltpu.SemaphoreType.DMA((3, 8)), pltpu.SemaphoreType.DMA((3, 8)), pltpu.SemaphoreType.DMA((4,))]
    fw, fwd, out, gout = pl.pallas_call(
        scatter_kernel, in_specs=[HBM] * 5, out_specs=[V, V, HBM, V],
        out_shape=[sds(2, rows // 2, D), sds(2, low // 2, D), sds(D, 2 * T), sds(8, D)],
        scratch_shapes=scratch,
        compiler_params=pltpu.CompilerParams(collective_id=2, has_side_effects=True, vmem_limit_bytes=50 * 2**20), name="scatter",
    )(gw.reshape(2, 4, 2, 2, 2, rows // 2, D), gwd.reshape(2, 4, 2, 2, 2, low // 2, D), out0, out1, gg)
    return fw.reshape(rows, D), fwd.reshape(low, D), out, gout


def shards(sizes, stream_pair, norm_gains, first_proj, down_proj, doc_lengths, pad_mask):
    s, d = lax.axis_index("section"), lax.axis_index("dp")
    sections, groups = sizes
    stream = jnp.pad(jnp.transpose(stream_pair, (2, 0, 1)).reshape(D - 1, -1), ((0, 1), (0, 0)))
    w = jnp.transpose(first_proj[0])
    wd = jnp.transpose(down_proj)
    gain = jnp.broadcast_to(norm_gains[0][:, None], (D, 128))
    whole = stream.shape[1]
    T = whole // sections
    nb = T // SLOTS
    own_docs = lax.dynamic_slice_in_dim(doc_lengths, s * nb, nb, axis=0)
    ends = jnp.stack([jnp.sum(own_docs[:, : j + 1], axis=1) for j in range(own_docs.shape[1])], axis=1)
    mask = lax.dynamic_slice_in_dim(pad_mask, s * T, T, axis=0).astype(f32)
    mask = jnp.broadcast_to(mask[None], (8, T))
    own_kernels = (sections, groups) == (2, 16)
    if own_kernels:
        weights, wd_full, x, g, gains = gather(w, wd, stream, gain)
    else:
        weights = lax.all_gather(lax.all_gather(w, "dp", axis=0, tiled=True), "section")
        wd_full = lax.all_gather(wd, ("section", "dp"), axis=0, tiled=True)
        both = lax.all_gather(stream, "section")
        x, g = lax.dynamic_slice_in_dim(both, s * T, T, axis=2)
        gains = lax.all_gather(gain, "section")
    qkv, att, lse, h0, x1, h1 = run_attn_fwd(ends, x, gains[0], gains[1], mask, weights[0])
    out1, dy, gw1, gwd, gg1 = run_ffn(g, gains[1], mask, x1, h1, weights[1], wd_full)
    out0, gw0, gg0 = run_attn_bwd(ends, x, gains[0], mask, weights[0], qkv, att, lse, h0, dy)
    gw = jnp.stack([gw0, gw1])
    gg = jnp.stack([gg0, gg1])
    if own_kernels:
        gg = jnp.broadcast_to(jnp.sum(gg, axis=2)[:, None], (2, 8, D))
        first, down, out, gain_total = scatter(gw, gwd, out0, out1, gg)
        gain_total = gain_total[0]
    else:
        first = lax.psum_scatter(gw.astype(f32), "section", scatter_dimension=0)
        first = lax.psum_scatter(first, "dp", scatter_dimension=0, tiled=True)
        down = lax.psum_scatter(gwd.astype(f32), ("section", "dp"), scatter_dimension=0, tiled=True)
        outs = lax.all_gather(jnp.stack([out0, out1]), "section")
        out = jnp.concatenate([lax.dynamic_index_in_dim(outs[i], s, 0, False) for i in range(2)], axis=1)
        gain_total = lax.psum_scatter(lax.psum(jnp.sum(gg, axis=2), "dp"), "section", scatter_dimension=0)
    share = D // groups
    gain_share = lax.dynamic_slice_in_dim(gain_total, d * share, share, axis=0)
    layer_out = jnp.transpose(out[: D - 1].reshape(D - 1, 1, whole), (1, 2, 0))
    return layer_out, gain_share[None], jnp.transpose(first)[None], jnp.transpose(down)


def solution(mesh):
    placed = (
        P("section", "dp", None),
        P("section", None),
        P("section", None, "dp"),
        P(None, ("section", "dp")),
        P("dp", None),
        P("dp"),
    )
    return jax.shard_map(
        functools.partial(shards, (mesh.shape["section"], mesh.shape["dp"])),
        mesh=mesh,
        in_specs=placed,
        out_specs=(
            P("section", "dp", None),
            P("section", "dp"),
            P("section", None, "dp"),
            P(None, ("section", "dp")),
        ),
        check_vma=False,
    )
```

time: 985 us -> 510 us (0.52); the launches traced: 970 us -> 510 us
  Pallas kernels: 0 us -> 460 us
  waiting for transfers between devices: 371 us -> 0 us
  matrix products: 157 us -> 0 us
  starting transfers between devices: 155 us -> 0 us
  local copies, waits for them, and re-layouts: 113 us -> 36.2 us
  other arithmetic: 79.5 us -> 12.7 us
  loops' own time: 46.9 us -> 0 us
  blocking collectives: 32.5 us -> 0 us
  between operations: 15.2 us -> 0.69 us
    pallas_call x0 -> x5, Pallas kernels: none -> 460 us  [the longest x1 177 us: gather(): pl.pallas_call(gather_kernel, in_specs=[HBM] * 4, out_specs=[HBM] * 5, ou...]
    reduce_scatter x2 -> x0, waiting for transfers between devices: 225 us -> none  [the longest x1 178 us: shards(): lax.psum_scatter(first_term, 'dp', scatter_dimension=1, tiled=True)]
    ppermute x11 -> x0, starting transfers between devices: 155 us -> none  [the longest x5 125 us: partner(): lax.ppermute(value, axis, [(i, i ^ 1 << bit) for i in range(lax.axis_size...]
    all_gather x2 -> x0, waiting for transfers between devices: 130 us -> none  [the longest x1 65.9 us: shards(): half_down = lax.all_gather(down_proj, 'dp', axis=1, tiled=True)]
    dot_general x19 -> x0, matrix products: 116 us -> none  [the longest x8 50.6 us: outer_cols(): lax.dot_general(left, right, (((1,), (1,)), ((), ())), preferred_element_...]
    another operation x6 -> x0, loops' own time: 46.9 us -> none  [shards(): lax.cond(on_attention, attention_side, mixer_side)]
    add x7 -> x0, other arithmetic: 46.5 us -> none  [the longest x3 32.6 us: shards(): totals = shares if totals is None else jax.tree.map(jnp.add, totals, shares)]
    cond x5 -> x0, matrix products: 40.8 us -> none  [shards(): lax.cond(on_attention, attention_side, mixer_side)]
  transfers between devices with their start and end apart: 15 -> 0, of which waited for: 8 -> 0; matrix products, arithmetic and copies ran while one was open for 16% -> 0% of each run, Pallas kernels for 0% -> 0%
where the time goes in v1:
time: 510 us
  Pallas kernels  460 us (90%)
  local copies, waits for them, and re-layouts  36.2 us (7%)
  other arithmetic  12.7 us (2%)
    pallas_call x1, Pallas kernels, gather(): pl.pallas_call(gather_kernel, in_specs=[HBM] * 4, out_specs=[HBM] * 5, ou...  177 us
    pallas_call x1, Pallas kernels, scatter(): pl.pallas_call(scatter_kernel, in_specs=[HBM] * 5, out_specs=[V, V, HBM,...  141 us
    pallas_call x1, Pallas kernels, run_ffn(): pl.pallas_call(ffn, in_specs=[V] * 7, out_specs=[V] * 5, out_shape=[sds(D...  52.9 us
    pallas_call x1, Pallas kernels, run_attn_bwd(): pl.pallas_call(attn_bwd, in_specs=[S] + [V] * 9, out_specs=[V] * 3, out_s...  51.3 us
    pallas_call x1, Pallas kernels, run_attn_fwd(): pl.pallas_call(attn_fwd, in_specs=[S] + [V] * 5, out_specs=[V] * 6, out_s...  37.8 us
    unnamed x8, local copies, waits for them, and re-layouts  16.9 us

profile of v1, /device:TPU:1, one launch (start us, length us, event | category | flops | bytes accessed | tf_op | source)
XLA Modules:
  0.0 509.9 jit_solution(18302865906014621732)
XLA Ops:
  0.6 0.8 fusion
  1.5 0.1 slice_reduce_fusion
  1.7 0.1 slice_reduce_fusion.1
  2.0 0.7 pad_add_fusion.ends_ref
  2.6 0.7 dynamic-slice_convert_fusion
  3.3 0.7 reduce
  4.0 0.6 broadcast_in_dim.12.mask_ref
  4.6 0.9 broadcast_in_dim.11.g_ref
  5.5 5.8 %copy.16 = f32[1,2048,767]{1,2,0:T(8,128)S(1)} copy(f32[1,2048,767]{1,0,2:T(1,128)} %param.6) | data formatting | bytes 12566528 | tf_op args[0]
  11.3 3.1 pad.4.s_ref
  14.5 177.4 %gather.1 = (bf16[2,4,2,2,2,96,768]{6,5,4,3,2,1,0:T(8,128)(2,1)}, bf16[2,4,2,2,2,48,768]{6,5,4,3,2,1,0:T(8,128)(2,1)}, f32[768,1024]{1,0:T(8,128)}, f32[768,1024]{1,0:T(8,128)}, f32[2,768,128]{2,1,0:T(8,128)}) custom-call(bf16[2,96,768]{2,1,0:T(8,128)(2,1)} %bitcast.53, bf16[2,48,768]{2,1,0:T(8,128)(2,1)} %bitcast.54, f32[768,2048]{1,0:T(8,128)} %pad.4.s_ref, ...), custom_call_target="tpu_custom_call" | custom-call | tf_op jit(solution)/shard_map/gather/pallas_call | solution.py:331
  191.8 2.1 slice_bitcast_fusion.2
  193.9 8.6 %fusion.1 = (bf16[1,4,2,2,2,96,768]{6,5,4,3,2,1,0:T(8,128)(2,1)}, bf16[1,4,2,2,2,96,768]{6,5,4,3,2,1,0:T(8,128)(2,1)}) fusion(bf16[2,4,2,2,2,96,768]{6,5,4,3,2,1,0:T(8,128)(2,1)} %get-tuple-element.29), kind=kLoop, calls=%fused_computation.13 | loop fusion | bytes 18874368 | tf_op jit(solution)/shard_map/slice | solution.py:463
  202.4 37.8 %attn_fwd.1 = (bf16[2304,1024]{1,0:T(8,128)(2,1)}, bf16[768,1024]{1,0:T(8,128)(2,1)}, f32[16,1024]{1,0:T(8,128)}, bf16[768,1024]{1,0:T(8,128)(2,1)}, f32[768,1024]{1,0:T(8,128)}, /*index=5*/bf16[768,1024]{1,0:T(8,128)(2,1)}) custom-call(s32[2,4]{1,0:T(2,128)} %pad_add_fusion.ends_ref, f32[768,1024]{1,0:T(8,128)} %get-tuple-element.27.x_ref, ...), custom_call_target="tpu_custom_call" | custom-call | tf_op jit(solution)/shard_map/attn_fwd/pallas_call | solution.py:214
  240.3 52.9 %ffn.1 = (f32[768,1024]{1,0:T(8,128)}, f32[768,1024]{1,0:T(8,128)}, bf16[3072,768]{1,0:T(8,128)(2,1)}, bf16[3072,768]{1,0:T(8,128)(2,1)}, f32[768,128]{1,0:T(8,128)}) custom-call(f32[768,1024]{1,0:T(8,128)} %get-tuple-element.34.g_ref, f32[768,128]{1,0:T(8,128)} %get-tuple-element.59.g1_ref, f32[8,1024]{1,0:T(8,128)} %broadcast_in_dim.12.mask_ref, ...), custom_call_target="tpu_custom_call" | custom-call | tf_op jit(solution)/shard_map/ffn/pallas_call | solution.py:220
  293.1 51.3 %attn_bwd.1 = (f32[768,1024]{1,0:T(8,128)}, bf16[3072,768]{1,0:T(8,128)(2,1)}, f32[768,128]{1,0:T(8,128)}) custom-call(s32[2,4]{1,0:T(2,128)} %pad_add_fusion.ends_ref, f32[768,1024]{1,0:T(8,128)} %get-tuple-element.27.x_ref, f32[768,128]{1,0:T(8,128)} %get-tuple-element.58.g0_ref, f32[8,1024]{1,0:T(8,128)} %broadcast_in_dim.12.mask_ref, ...), custom_call_target="tpu_custom_call" | custom-call | tf_op jit(solution)/shard_map/attn_bwd/pallas_call | solution.py:227
  344.4 1.3 maximum_reduce_fusion
  345.7 8.4 %pad_maximum_fusion.gw = bf16[2,4,2,2,2,96,768]{6,5,4,3,2,1,0:T(8,128)(2,1)} fusion(bf16[1,4,2,2,2,96,768]{6,5,4,3,2,1,0:T(8,128)(2,1)} %bitcast.49, bf16[1,4,2,2,2,96,768]{6,5,4,3,2,1,0:T(8,128)(2,1)} %bitcast.50), kind=kLoop, calls=%fused_computation | loop fusion | flops 4718592 | bytes 18874368 | tf_op jit(solution)/shard_map/stack | solution.py:465
  354.1 141.0 %scatter.1 = (f32[2,96,768]{2,1,0:T(8,128)S(1)}, f32[2,48,768]{2,1,0:T(8,128)S(1)}, f32[768,2048]{1,0:T(8,128)}, f32[8,768]{1,0:T(8,128)S(1)}) custom-call(bf16[2,4,2,2,2,96,768]{6,5,4,3,2,1,0:T(8,128)(2,1)} %pad_maximum_fusion.gw, bf16[2,4,2,2,2,48,768]{6,5,4,3,2,1,0:T(8,128)(2,1)} %bitcast.47, f32[768,1024]{1,0:T(8,128)S(1)} %copy-done, ...), custom_call_target="tpu_custom_call" | custom-call | tf_op jit(solution)/shard_map/scatter/pallas_call | solution.py:430
  495.1 3.2 slice_bitcast_fusion
  498.3 9.5 %copy.14 = f32[1,2048,767]{1,0,2:T(1,128)} copy(f32[1,2048,767]{1,2,0:T(8,128)S(1)} %slice_bitcast_fusion) | data formatting | bytes 12566528
  507.8 0.6 constant_dynamic-slice_fusion
  508.4 0.8 copy.19
  509.2 0.7 copy.20
  (9 shorter events, 0.3 us)
Async XLA Ops:
  293.1 51.3 %copy-start.1 = (f32[768,128]{1,0:T(8,128)S(1)}, f32[768,128]{1,0:T(8,128)}, u32[]{:S(2)}) copy-start(f32[768,128]{1,0:T(8,128)} %get-tuple-element.45) | copy-start | bytes 1179652
  345.7 8.4 %copy-start = (f32[768,1024]{1,0:T(8,128)S(1)}, f32[768,1024]{1,0:T(8,128)}, u32[]{:S(2)}) copy-start(f32[768,1024]{1,0:T(8,128)} %get-tuple-element.42.o0) | copy-start | bytes 9437188

commit v2 on v1

v2 whole, which is shorter than its diff:
```python
import functools
import jax, jax.numpy as jnp
from jax import lax
from jax.experimental import pallas as pl
from jax.experimental.pallas import tpu as pltpu
from jax.sharding import PartitionSpec as P

HEADS, HEAD_DIM, FF, D, SLOTS = 12, 64, 3072, 768, 512
LONGEST = 256
EPS, MASKED = 1e-05, -1e30
VMEM_MOST = 63 * 2**20
f32, bf16 = jnp.float32, jnp.bfloat16
CHUNK = 768

def nn(a, b):
    return lax.dot_general(a, b, (((1,), (0,)), ((), ())), preferred_element_type=f32)
def nt(a, b):
    return lax.dot_general(a, b, (((1,), (1,)), ((), ())), preferred_element_type=f32)
def tn(a, b):
    return lax.dot_general(a, b, (((0,), (0,)), ((), ())), preferred_element_type=f32)

def last_row(shape):
    return lax.broadcasted_iota(jnp.int32, shape, 0) == shape[0] - 1

def expanded(x):
    return jnp.where(last_row(x.shape), -jnp.sum(x, axis=0, keepdims=True), x)

def inv_rms(x):
    return lax.rsqrt(jnp.mean(x * x, axis=0, keepdims=True) + EPS)

def bias_block(ends, live, first_key, keys, first_query, queries):
    shape = (keys, queries)
    kp = lax.broadcasted_iota(jnp.int32, shape, 0) + first_key
    qp = lax.broadcasted_iota(jnp.int32, shape, 1) + first_query
    kd = sum((kp >= e).astype(jnp.int32) for e in ends)
    qd = sum((qp >= e).astype(jnp.int32) for e in ends)
    seen = (kd == qd) & (kp <= qp) & ((live > 0.5) | (kp == qp))
    return jnp.where(seen, 0.0, MASKED)

def attn_fwd(ends_ref, x_ref, g0_ref, g1_ref, mask_ref, w_ref,
             qkv_ref, att_ref, lse_ref, h0_ref, x1_ref, h1_ref, bias_ref):
    T = x_ref.shape[1]
    nb = T // SLOTS
    @pl.loop(0, T // 256)
    def _(t):
        c = pl.ds(pl.multiple_of(t * 256, 256), 256)
        x = expanded(x_ref[:, c])
        h0_ref[:, c] = (x * inv_rms(x) * g0_ref[:, :1]).astype(bf16)
    for b in range(nb):
        ends = [ends_ref[b, j] for j in range(3)]
        marks = jnp.broadcast_to(mask_ref[:1, b * SLOTS:(b + 1) * SLOTS], (128, SLOTS)).T
        for qb in range(2):
            nk = 256 * (qb + 1)
            for q0 in (0, 128):
                bias_ref[b, :nk, qb * 256 + q0: qb * 256 + q0 + 128] = bias_block(ends, marks[:nk], 0, nk, qb * 256 + q0, 128)
    @pl.loop(0, 9)
    def _(m):
        r = pl.ds(pl.multiple_of(m * 256, 256), 256)
        qkv_ref[r, :] = nn(w_ref[r, :], h0_ref[...]).astype(bf16)
    for b in range(nb):
        cols = slice(b * SLOTS, (b + 1) * SLOTS)
        @pl.loop(0, HEADS // 2)
        def _(hp):
            for hh in range(2):
                h = hp * 2 + hh
                off = pl.multiple_of(h * HEAD_DIM, HEAD_DIM)
                q = qkv_ref[pl.ds(off, HEAD_DIM), cols] * bf16(HEAD_DIM ** -0.5)
                k = qkv_ref[pl.ds(off + D, HEAD_DIM), cols].T
                v = qkv_ref[pl.ds(off + 2 * D, HEAD_DIM), cols]
                for qb in range(2):
                    nk, lo = 256 * (qb + 1), qb * 256
                    s = nn(k[:nk], q[:, lo:lo + 256]) + bias_ref[b, :nk, lo:lo + 256]
                    mx = jnp.max(s, axis=0, keepdims=True)
                    p = jnp.exp(s - mx)
                    tot = jnp.sum(p, axis=0, keepdims=True)
                    lse_ref[pl.ds(h, 1), b * SLOTS + lo: b * SLOTS + lo + 256] = mx + jnp.log(tot)
                    low = (p * (1.0 / tot)).astype(bf16)
                    att_ref[pl.ds(off, HEAD_DIM), b * SLOTS + lo: b * SLOTS + lo + 256] = nn(v[:, :nk], low).astype(bf16)
    @pl.loop(0, T // 256)
    def _(t):
        c = pl.ds(pl.multiple_of(t * 256, 256), 256)
        x = expanded(x_ref[:, c])
        a = nn(w_ref[3 * D:, :], att_ref[:, c])
        x1 = expanded(jnp.where(last_row(x.shape), 0.0, x + (a - jnp.mean(a, axis=0, keepdims=True))))
        x1_ref[:, c] = x1
        h1_ref[:, c] = (x1 * inv_rms(x1) * g1_ref[:, :1]).astype(bf16)

C0 = 0.7978845608028654
def gelu_both(u):
    u2 = u * u
    inner = C0 * u * (1.0 + 0.044715 * u2)
    t = jnp.tanh(inner)
    half = 0.5 * (1.0 + t)
    slope = half + 0.5 * u * (1.0 - t * t) * (C0 * (1.0 + 3 * 0.044715 * u2))
    return u * half, slope

def norm_back(x, r, gain, dh):
    e = gain * dh
    dx = r * e - x * (r * r * r) * jnp.mean(x * e, axis=0, keepdims=True)
    return dx, dh * x * r

def lane_fold(v):
    return sum(v[:, i * 128:(i + 1) * 128] for i in range(v.shape[1] // 128))

def ffn(g_ref, g1_ref, mask_ref, x1_ref, h1_ref, w1_ref, wd_ref,
        out1_ref, dy_ref, gw1_ref, gwd_ref, gg_ref, dm_ref, z_ref, du_ref, u_ref, macc, hacc):
    T = g_ref.shape[1]
    nt_ = T // 256
    @pl.loop(0, nt_)
    def _(t):
        c = pl.ds(pl.multiple_of(t * 256, 256), 256)
        g = g_ref[:, c] * mask_ref[:1, c]
        dm_ref[:, c] = (g - jnp.mean(g, axis=0, keepdims=True)).astype(bf16)
    macc[...] = jnp.zeros_like(macc)
    hacc[...] = jnp.zeros_like(hacc)
    @pl.loop(0, FF // CHUNK)
    def _(p):
        base = p * CHUNK
        @pl.loop(0, CHUNK // 256)
        def _(m):
            r = pl.ds(pl.multiple_of(base + m * 256, 256), 256)
            rl = pl.ds(pl.multiple_of(m * 256, 256), 256)
            for n in range(T // 512):
                cs = slice(n * 512, (n + 1) * 512)
                z, slope = gelu_both(nn(w1_ref[r, :], h1_ref[:, cs]))
                z_ref[rl, cs] = z.astype(bf16)
                du_ref[rl, cs] = (nn(wd_ref[r, :], dm_ref[:, cs]) * slope).astype(bf16)
        rows = pl.ds(pl.multiple_of(base, CHUNK), CHUNK)
        @pl.loop(0, 3)
        def _(m):
            o = pl.ds(pl.multiple_of(m * 256, 256), 256)
            macc[o, :] += tn(wd_ref[rows, o], z_ref[...])
            hacc[o, :] += tn(w1_ref[rows, o], du_ref[...])
            r = pl.ds(pl.multiple_of(base + m * 256, 256), 256)
            gw1_ref[r, :] = nt(du_ref[o, :], h1_ref[...]).astype(gw1_ref.dtype)
            gwd_ref[r, :] = nt(z_ref[o, :], dm_ref[...]).astype(gwd_ref.dtype)
    gg_ref[...] = jnp.zeros_like(gg_ref)
    @pl.loop(0, nt_)
    def _(t):
        c = pl.ds(pl.multiple_of(t * 256, 256), 256)
        x1, m = x1_ref[:, c], macc[:, c]
        out1_ref[:, c] = x1 + (m - jnp.mean(m, axis=0, keepdims=True))
        g = g_ref[:, c] * mask_ref[:1, c]
        dx, gg = norm_back(x1, inv_rms(x1), g1_ref[:, :1], hacc[:, c])
        gg_ref[...] += lane_fold(gg)
        dy_ref[:, c] = g + dx - dx[D - 1:, :]

def attn_bwd(ends_ref, x_ref, g0_ref, mask_ref, w_ref, qkv_ref, att_ref, lse_ref, h0_ref, dy_ref,
             out0_ref, gw_ref, gg_ref, da_ref, dat_ref, dqkv_ref, bias_ref):
    T = x_ref.shape[1]
    nb = T // SLOTS
    for b in range(nb):
        ends = [ends_ref[b, j] for j in range(3)]
        marks = jnp.broadcast_to(mask_ref[:1, b * SLOTS:(b + 1) * SLOTS], (128, SLOTS)).T
        for qb in range(2):
            nk = 256 * (qb + 1)
            for q0 in (0, 128):
                bias_ref[b, :nk, qb * 256 + q0: qb * 256 + q0 + 128] = bias_block(ends, marks[:nk], 0, nk, qb * 256 + q0, 128)
    @pl.loop(0, T // 256)
    def _(t):
        c = pl.ds(pl.multiple_of(t * 256, 256), 256)
        dy = dy_ref[:, c]
        da_ref[:, c] = (dy - jnp.mean(dy, axis=0, keepdims=True)).astype(bf16)
    @pl.loop(0, 3)
    def _(m):
        o = pl.ds(pl.multiple_of(m * 256, 256), 256)
        r = pl.ds(pl.multiple_of(3 * D + m * 256, 256), 256)
        gw_ref[r, :] = nt(da_ref[o, :], att_ref[...]).astype(gw_ref.dtype)
        dat_ref[o, :] = tn(w_ref[3 * D:, o], da_ref[...]).astype(bf16)
    for b in range(nb):
        cols = slice(b * SLOTS, (b + 1) * SLOTS)
        @pl.loop(0, HEADS)
        def _(h):
            off = pl.multiple_of(h * HEAD_DIM, HEAD_DIM)
            q = qkv_ref[pl.ds(off, HEAD_DIM), cols] * bf16(HEAD_DIM ** -0.5)
            kt = qkv_ref[pl.ds(off + D, HEAD_DIM), cols]
            k = kt.T
            v = qkv_ref[pl.ds(off + 2 * D, HEAD_DIM), cols].T
            d = dat_ref[pl.ds(off, HEAD_DIM), cols]
            dks, dvs = [], []
            for qb in range(2):
                nk, lo = 256 * (qb + 1), qb * 256
                s = nn(k[:nk], q[:, lo:lo + 256]) + bias_ref[b, :nk, lo:lo + 256]
                p = jnp.exp(s - lse_ref[pl.ds(h, 1), b * SLOTS + lo: b * SLOTS + lo + 256])
                dp = nn(v[:nk], d[:, lo:lo + 256])
                ds = (p * (dp - jnp.sum(p * dp, axis=0, keepdims=True))).astype(bf16)
                low = p.astype(bf16)
                dqkv_ref[pl.ds(off, HEAD_DIM), b * SLOTS + lo: b * SLOTS + lo + 256] = (nn(kt[:, :nk], ds) * HEAD_DIM ** -0.5).astype(bf16)
                dks.append(nt(q[:, lo:lo + 256], ds))
                dvs.append(nt(d[:, lo:lo + 256], low))
            for at, parts in ((D, dks), (2 * D, dvs)):
                dqkv_ref[pl.ds(off + at, HEAD_DIM), b * SLOTS: b * SLOTS + 256] = (parts[0] + parts[1][:, :256]).astype(bf16)
                dqkv_ref[pl.ds(off + at, HEAD_DIM), b * SLOTS + 256: (b + 1) * SLOTS] = parts[1][:, 256:].astype(bf16)
    @pl.loop(0, 9)
    def _(m):
        r = pl.ds(pl.multiple_of(m * 256, 256), 256)
        gw_ref[r, :] = nt(dqkv_ref[r, :], h0_ref[...]).astype(gw_ref.dtype)
    gg_ref[...] = jnp.zeros_like(gg_ref)
    @pl.loop(0, T // 256)
    def _(t):
        c = pl.ds(pl.multiple_of(t * 256, 256), 256)
        x = expanded(x_ref[:, c])
        dh = tn(w_ref[:3 * D, :], dqkv_ref[:, c])
        dx, gg = norm_back(x, inv_rms(x), g0_ref[:, :1], dh)
        gg_ref[...] += lane_fold(gg)
        out0_ref[:, c] = dy_ref[:, c] + dx - dx[D - 1:, :]

V = pl.BlockSpec(memory_space=pltpu.VMEM)
S = pl.BlockSpec(memory_space=pltpu.SMEM)
def sds(*shape, dtype=f32):
    return jax.ShapeDtypeStruct(shape, dtype)
PARAMS = pltpu.CompilerParams(vmem_limit_bytes=60 * 2**20)

def run_attn_fwd(ends, x, g0, g1, mask, w):
    T = x.shape[1]
    return pl.pallas_call(attn_fwd, in_specs=[S] + [V] * 5, out_specs=[V] * 6,
        out_shape=[sds(3 * D, T, dtype=bf16), sds(D, T, dtype=bf16), sds(16, T), sds(D, T, dtype=bf16), sds(D, T), sds(D, T, dtype=bf16)],
        scratch_shapes=[pltpu.VMEM((T // SLOTS, SLOTS, SLOTS), f32)], compiler_params=PARAMS, name="attn_fwd")(ends, x, g0, g1, mask, w)

def run_ffn(g, g1, mask, x1, h1, w1, wd, gdt=bf16):
    T = g.shape[1]
    return pl.pallas_call(ffn, in_specs=[V] * 7, out_specs=[V] * 5,
        out_shape=[sds(D, T), sds(D, T), sds(FF, D, dtype=gdt), sds(FF, D, dtype=gdt), sds(D, 128)],
        scratch_shapes=[pltpu.VMEM((D, T), bf16), pltpu.VMEM((CHUNK, T), bf16), pltpu.VMEM((CHUNK, T), bf16), pltpu.VMEM((8, 128), f32), pltpu.VMEM((D, T), f32), pltpu.VMEM((D, T), f32)],
        compiler_params=PARAMS, name="ffn")(g, g1, mask, x1, h1, w1, wd)

def run_attn_bwd(ends, x, g0, mask, w, qkv, att, lse, h0, dy, gdt=bf16):
    T = x.shape[1]
    return pl.pallas_call(attn_bwd, in_specs=[S] + [V] * 9, out_specs=[V] * 3,
        out_shape=[sds(D, T), sds(FF, D, dtype=gdt), sds(D, 128)],
        scratch_shapes=[pltpu.VMEM((D, T), bf16), pltpu.VMEM((D, T), bf16), pltpu.VMEM((3 * D, T), bf16), pltpu.VMEM((T // SLOTS, SLOTS, SLOTS), f32)],
        compiler_params=PARAMS, name="attn_bwd")(ends, x, g0, mask, w, qkv, att, lse, h0, dy)


MESH = pl.DeviceIdType.MESH
HBM = pl.BlockSpec(memory_space=pl.ANY)


def push(src, dst, send, recv, device):
    copy = pltpu.make_async_remote_copy(
        src_ref=src, dst_ref=dst, send_sem=send, recv_sem=recv, device_id=device, device_id_type=MESH
    )
    copy.start()
    return copy


DIST = (0, 1, 3, 2)
TILE = 256
SCALE = HEAD_DIM ** -0.5
KIND_A, KIND_D, KIND_W = 0, 1, 2
SETS = 12
PLANES = (3, 0, 1, 2)


def wide(v):
    return v.astype(f32)


def square(v):
    return v.reshape(-1, D)


def at_step(k):
    return (1 - k // 2) * k + (k // 2) * (5 - k)


def layer_kernel(
    len_ref, mask_ref, gain_ref, stream, w_ref, wd_ref,
    out, first, down, gain_out, spill_x, spill_q,
    fa, fw, fd, X, G, xt, gt, QKV, ATT, H0, H1, DM, MACC, HACC, BIAS, LSE, MK, GR, GCOL, GG, GV, GL, GT,
    STG, ACC, L1, L2, L3W, L3A, L3D, FIN, FIND,
    zs, zr, ps, pr, ss, sr, p1s, p1r, p2s, p2r, p3s, rw, ra, rd, i_s, i_r, local, gs, gr,
):
    s, d = lax.axis_index("section"), lax.axis_index("dp")
    x, y, z, xy = lax.rem(d, 2), lax.rem(d // 2, 2), d // 4, lax.rem(d, 4)
    t = 1 - s
    over_y, over_x = (1 - y) * 2 + x, y * 2 + 1 - x
    xy1, xy2, xy3 = t * over_y + s * over_x, s * over_y + t * over_x, 3 - xy
    sib, n1, n2 = (t, d), (s, z * 4 + xy1), (s, z * 4 + xy2)
    T = X.shape[1]
    nb = T // SLOTS
    tiles = T // TILE
    col = lambda i: pl.ds(pl.multiple_of(i * TILE, TILE), TILE)
    at_plane = lambda p: (s, p * 4 + xy)

    def plane(i):
        return lax.rem(z + 4 - DIST[i], 4)

    def wait_recv(dst, sem):
        pltpu.make_async_remote_copy(
            src_ref=dst, dst_ref=dst, send_sem=sem, recv_sem=sem, device_id=sib, device_id_type=MESH
        ).wait_recv()

    def wait_send(src, sem):
        pltpu.make_async_remote_copy(
            src_ref=src, dst_ref=src, send_sem=sem, recv_sem=sem, device_id=sib, device_id_type=MESH
        ).wait_send()

    def move(src, dst, sem):
        pltpu.make_async_copy(src, dst, sem).start()

    def moved(src, dst, sem):
        pltpu.make_async_copy(src, dst, sem).wait()

    def slab(kind, zz, q, h):
        return fd.at[:, zz, q, h] if kind == KIND_D else (fa, None, fw)[kind].at[zz, q, h]

    def group(kind, zz, h):
        return fd.at[:, zz, :, h] if kind == KIND_D else (fa, None, fw)[kind].at[zz, :, h]

    def Z(kind, i):
        own = slab(kind, z, xy, s)
        push(own, own, zs.at[kind, i], zr.at[kind, i], at_plane(lax.rem(z + DIST[i], 4)))

    def A(kind, i):
        here = slab(kind, plane(i), xy, s)
        if i:
            wait_recv(here, zr.at[kind, i])
        if 0 < i < 3:
            Z(kind, i + 1)
        elif i == 3 and kind < 2:
            Z(kind + 1, 1)
        push(here, here, ps.at[kind, i, 0], pr.at[kind, i, 0], n1)
        push(here, here, ps.at[kind, i, 1], pr.at[kind, i, 1], n2)

    def B(kind, i):
        here = slab(kind, plane(i), xy1, s)
        wait_recv(here, pr.at[kind, i, 0])
        push(here, here, ps.at[kind, i, 2], pr.at[kind, i, 2], n2)

    def C(kind, i):
        zz = plane(i)
        wait_recv(slab(kind, zz, xy2, s), pr.at[kind, i, 1])
        wait_recv(slab(kind, zz, xy3, s), pr.at[kind, i, 2])
        here = group(kind, zz, s)
        push(here, here, ps.at[kind, i, 3], pr.at[kind, i, 3], sib)

    def E(kind, i):
        wait_recv(group(kind, plane(i), t), pr.at[kind, i, 3])

    def sent(kind):
        for i in range(4):
            zz = plane(i)
            if i:
                wait_send(slab(kind, z, xy, s), zs.at[kind, i])
            wait_send(slab(kind, zz, xy, s), ps.at[kind, i, 0])
            wait_send(slab(kind, zz, xy, s), ps.at[kind, i, 1])
            wait_send(slab(kind, zz, xy1, s), ps.at[kind, i, 2])
            wait_send(group(kind, zz, s), ps.at[kind, i, 3])

    def to_sibling(j):
        push(STG.at[j % 2 if isinstance(j, int) else lax.rem(j, 2), :, t], ACC.at[j], ss.at[j], sr.at[j], sib)

    def staged_free(j):
        wait_send(STG.at[0, :, t], ss.at[j])

    def R1(j):
        wait_recv(ACC.at[j], sr.at[j])
        for q in range(4):
            ACC[j, q] = (wide(ACC[j, q]) + wide(STG[j % 2, q, s])).astype(bf16)
        push(ACC.at[j, xy2], L1.at[j, 0], p1s.at[j, 0], p1r.at[j, 0], n2)
        push(ACC.at[j, xy3], L1.at[j, 1], p1s.at[j, 1], p1r.at[j, 1], n2)

    def R2(j):
        wait_recv(L1.at[j, 0], p1r.at[j, 0])
        wait_recv(L1.at[j, 1], p1r.at[j, 1])
        ACC[j, xy] = (wide(ACC[j, xy]) + wide(L1[j, 0])).astype(bf16)
        ACC[j, xy1] = (wide(ACC[j, xy1]) + wide(L1[j, 1])).astype(bf16)
        push(ACC.at[j, xy1], L2.at[j], p2s.at[j], p2r.at[j], n1)

    def ends_of(j):
        if j >= 8:
            p = PLANES[j - 8]
            return [(z != p, ACC.at[j, xy], L3A.at[z], p3s.at[j, 0], ra.at[z], p)]
        k = j // 2
        p = plane(k)
        if j % 2 == 0:
            return [(None, ACC.at[j, xy], L3W.at[k - 1], p3s.at[j, 0], rw.at[k - 1], p)] if k else []
        made = []
        for sub in range(2):
            to = 2 * lax.rem(p, 2) + sub
            made.append((z != to, ACC.at[j, xy, sub], L3D.at[p // 2, z], p3s.at[j, sub], rd.at[p // 2, z], to))
        return made

    def guarded(cond, act):
        act() if cond is None else pl.when(cond)(act)

    def R3(j):
        wait_recv(L2.at[j], p2r.at[j])
        ACC[j, xy] = (wide(ACC[j, xy]) + wide(L2[j])).astype(bf16)
        for cond, src, dst, ssem, rsem, to in ends_of(j):
            guarded(cond, lambda src=src, dst=dst, ssem=ssem, rsem=rsem, to=to: push(src, dst, ssem, rsem, at_plane(to)) and None)

    def scattered(j):
        wait_send(ACC.at[j, xy2], p1s.at[j, 0])
        wait_send(ACC.at[j, xy3], p1s.at[j, 1])
        wait_send(ACC.at[j, xy1], p2s.at[j])
        for cond, src, dst, ssem, rsem, to in ends_of(j):
            guarded(cond, lambda src=src, ssem=ssem: wait_send(src, ssem))

    barrier = pltpu.get_barrier_semaphore()
    partners = [sib, n1, n2, *(at_plane(lax.rem(z + r, 4)) for r in (1, 2, 3))]
    for device in partners:
        pl.semaphore_signal(barrier, inc=1, device_id=device, device_id_type=MESH)
    pl.semaphore_wait(barrier, len(partners))

    mine, other = pl.ds(pl.multiple_of(s * T, T), T), pl.ds(pl.multiple_of(t * T, T), T)
    top = pl.ds(0, D - 8)

    def rows_of(part):
        return stream.at[top, 0, part], stream.at[pl.ds(D - 9, 8), 0, part]

    @pl.when(s == 0)
    def _():
        push(w_ref.at[1], fa.at[z, xy, 1], i_s.at[0], i_r.at[0], sib)
        move(w_ref.at[0], fa.at[z, xy, 0], local.at[0])

    @pl.when(s == 1)
    def _():
        push(w_ref.at[0], fw.at[z, xy, 0], i_s.at[0], i_r.at[0], sib)
        move(w_ref.at[1], fw.at[z, xy, 1], local.at[0])

    push(wd_ref.at[t], fd.at[s, z, xy, t], i_s.at[1], i_r.at[1], sib)
    move(wd_ref.at[s], fd.at[s, z, xy, s], local.at[1])
    push(gain_ref, GR.at[s], i_s.at[2], i_r.at[2], sib)
    move(gain_ref, GR.at[s], local.at[2])

    def stream_in(keep, tail):
        def go():
            a, b = rows_of(mine)
            move(a, keep.at[top], local.at[3])
            move(b, tail, local.at[4])
        return go

    def stream_out(give, tail):
        def go():
            a, b = rows_of(other)
            push(a, give.at[top], i_s.at[3], i_r.at[3], sib)
            push(b, tail, i_s.at[4], i_r.at[4], sib)
        return go

    pl.when(s == 0)(stream_in(X, xt))
    pl.when(s == 1)(stream_in(G, gt))

    @pl.when(s == 0)
    def _():
        moved(w_ref.at[0], fa.at[z, xy, 0], local.at[0])
        wait_send(w_ref.at[1], i_s.at[0])

    @pl.when(s == 1)
    def _():
        wait_recv(fa.at[z, xy, 1], i_r.at[0])

    Z(KIND_A, 1)
    A(KIND_A, 0)
    pl.when(s == 0)(stream_out(X, xt))
    pl.when(s == 1)(stream_out(G, gt))

    def lengths(b):
        return [len_ref[s * nb + b, j] for j in range(4)]

    shifts, ends = [], []
    for b in range(nb):
        size = lengths(b)
        stops = [size[0], size[0] + size[1], size[0] + size[1] + size[2]]
        starts = [0, *stops]
        shifts.append(sum(jnp.where(size[j] == LONGEST, starts[j], 0) for j in range(1, 4)))
        ends.append(stops)

    moved(gain_ref, GR.at[s], local.at[2])
    wait_recv(GR.at[t], i_r.at[2])
    for j in range(2):
        GCOL[j] = jnp.broadcast_to(GR[j], (128, D)).T

    def turn(ref, tail, b):
        cols = slice(b * SLOTS, (b + 1) * SLOTS)
        amount = lax.rem(SLOTS - shifts[b], SLOTS)
        ref[D - 8:, cols] = jnp.concatenate([tail[1:, cols], jnp.zeros((1, SLOTS), f32)], axis=0)

        @pl.loop(0, 8)
        def _(i):
            r = pl.ds(pl.multiple_of(i * 96, 96), 96)
            ref[r, cols] = pltpu.roll(ref[r, cols], amount, 1)

    def x_arrived():
        @pl.when(s == 0)
        def _():
            a, b = rows_of(mine)
            moved(a, X.at[top], local.at[3])
            moved(b, xt, local.at[4])

        @pl.when(s == 1)
        def _():
            wait_recv(X.at[top], i_r.at[3])
            wait_recv(xt, i_r.at[4])

    def g_arrived():
        @pl.when(s == 1)
        def _():
            a, b = rows_of(mine)
            moved(a, G.at[top], local.at[3])
            moved(b, gt, local.at[4])

        @pl.when(s == 0)
        def _():
            wait_recv(G.at[top], i_r.at[3])
            wait_recv(gt, i_r.at[4])

    def masks():
        for b in range(nb):
            cols = slice(b * SLOTS, (b + 1) * SLOTS)
            amount = lax.rem(SLOTS - shifts[b], SLOTS)
            live = wide(mask_ref[:, pl.ds(pl.multiple_of(s * T + b * SLOTS, SLOTS), SLOTS)])
            MK[:, cols] = pltpu.roll(jnp.broadcast_to(live, (8, SLOTS)), amount, 1)
            marks = jnp.broadcast_to(MK[:1, cols], (128, SLOTS)).T
            for qb in range(2):
                for half in range(2):
                    shape = (TILE, 128)
                    kp = lax.broadcasted_iota(jnp.int32, shape, 0) + qb * TILE
                    qp = lax.broadcasted_iota(jnp.int32, shape, 1) + qb * TILE + half * 128

                    def doc(p):
                        first_place = p + shifts[b]
                        first_place = first_place - jnp.where(first_place >= SLOTS, SLOTS, 0)
                        return sum((first_place >= e).astype(jnp.int32) for e in ends[b])

                    seen = (doc(kp) == doc(qp)) & (kp <= qp)
                    seen = seen & ((marks[qb * TILE:(qb + 1) * TILE] > 0.5) | (kp == qp))
                    BIAS[b, qb, :, half * 128:(half + 1) * 128] = jnp.where(seen, 0.0, MASKED)

    def normed_in():
        @pl.loop(0, tiles)
        def _(i):
            c = col(i)
            v = expanded(X[:, c])
            X[D - 8:, c] = v[D - 8:]
            H0[:, c] = (v * inv_rms(v) * GCOL[0, :, :1]).astype(bf16)

    def cotangent():
        @pl.loop(0, tiles)
        def _(i):
            c = col(i)
            v = G[:, c] * MK[:1, c]
            G[:, c] = v
            DM[:, c] = (v - jnp.mean(v, axis=0, keepdims=True)).astype(bf16)

    masks()
    B(KIND_A, 0)
    x_arrived()
    turn(X, xt, 0)
    A(KIND_A, 1)
    turn(X, xt, 1)
    C(KIND_A, 0)
    normed_in()
    move(X, spill_x, local.at[5])
    B(KIND_A, 1)
    A(KIND_A, 2)

    @pl.when(s == 0)
    def _():
        wait_recv(fw.at[z, xy, 0], i_r.at[0])

    @pl.when(s == 1)
    def _():
        moved(w_ref.at[1], fw.at[z, xy, 1], local.at[0])
        wait_send(w_ref.at[0], i_s.at[0])

    moved(wd_ref.at[s], fd.at[s, z, xy, s], local.at[1])
    wait_recv(fd.at[t, z, xy, s], i_r.at[1])
    C(KIND_A, 1)
    B(KIND_A, 2)
    g_arrived()
    turn(G, gt, 0)
    A(KIND_A, 3)
    turn(G, gt, 1)
    C(KIND_A, 2)
    cotangent()
    B(KIND_A, 3)
    A(KIND_D, 0)
    C(KIND_A, 3)
    for i in range(4):
        E(KIND_A, i)

    def ticks(index, table):
        for at, steps in table.items():
            @pl.when(index == at)
            def _(steps=steps):
                for act, *args in steps:
                    act(*args)

    @pl.loop(0, 3)
    def _(p):
        rows = pl.ds(pl.multiple_of(p * D, D), D)
        QKV[rows, :] = nn(square(fa[p]), H0[...]).astype(bf16)
        ticks(p, {0: [(B, KIND_D, 0)], 2: [(A, KIND_D, 1)]})

    units = [(h, qb) for h in range(4) for qb in range(2)]

    def spots(i):
        b = i // 3
        def spot(u):
            head = lax.rem(i, 3) * 4 + u[0]
            return head, pl.multiple_of(head * HEAD_DIM, HEAD_DIM), pl.ds(pl.multiple_of(b * SLOTS + u[1] * TILE, TILE), TILE)
        return b, spot

    def three(off, c):
        return [QKV[pl.ds(off + j * D, HEAD_DIM), c] for j in range(3)]

    @pl.loop(0, 3 * nb)
    def _(i):
        b, spot = spots(i)
        scores, probs = {}, {}
        for u in units:
            head, off, c = spot(u)
            q, k, v = three(off, c)
            scores[u] = nn(k.T, q * bf16(SCALE))
        for u in units:
            head, off, c = spot(u)
            v = scores[u] + BIAS[b, u[1]]
            highest = jnp.max(v, axis=0, keepdims=True)
            p = jnp.exp(v - highest)
            total = jnp.sum(p, axis=0, keepdims=True)
            LSE[pl.ds(head, 1), c] = highest + jnp.log(total)
            probs[u] = (p * (1.0 / total)).astype(bf16)
        for u in units:
            head, off, c = spot(u)
            ATT[pl.ds(off, HEAD_DIM), c] = nn(QKV[pl.ds(off + 2 * D, HEAD_DIM), c], probs[u]).astype(bf16)
        ticks(i, {0: [(C, KIND_D, 0)], 1: [(B, KIND_D, 1)], 3: [(A, KIND_D, 2), (C, KIND_D, 1)], 5: [(B, KIND_D, 2)]})

    move(QKV, spill_q, local.at[6])
    moved(X, spill_x, local.at[5])

    @pl.loop(0, tiles)
    def _(i):
        c = col(i)
        a = nn(square(fa[3]), ATT[:, c])
        v = X[:, c] + (a - jnp.mean(a, axis=0, keepdims=True))
        v = expanded(jnp.where(last_row(v.shape), 0.0, v))
        X[:, c] = v
        H1[:, c] = (v * inv_rms(v) * GCOL[1, :, :1]).astype(bf16)
        ticks(i, {1: [(A, KIND_D, 3)], 2: [(C, KIND_D, 2)], 3: [(B, KIND_D, 3)]})

    MACC[...] = jnp.zeros_like(MACC)
    HACC[...] = jnp.zeros_like(HACC)
    moved(QKV, spill_q, local.at[6])
    A(KIND_W, 0)
    C(KIND_D, 3)
    for i in range(4):
        E(KIND_D, i)
    B(KIND_W, 0)
    A(KIND_W, 1)
    C(KIND_W, 0)
    B(KIND_W, 1)
    E(KIND_W, 0)
    ZT, DU = QKV.at[pl.ds(0, D)], QKV.at[pl.ds(D, D)]

    def stage_rows(slot, left, right, by_plane):
        for m in range(2):
            v = nt(left(m), right).astype(bf16)
            if by_plane:
                for a in range(2):
                    for h in range(2):
                        for sub in range(2):
                            lo = a * 192 + h * 96 + sub * 48
                            STG[slot, 2 * m + a, h, sub] = v[lo:lo + 48]
            else:
                for q in range(4):
                    for h in range(2):
                        STG[slot, q, h, m] = v[q * 96 + h * 48:q * 96 + h * 48 + 48]

    FFN_TICKS = {
        (0, "a1"): [(A, KIND_W, 2)], (0, "a2"): [(C, KIND_W, 1)], (0, "a3"): [(B, KIND_W, 2)],
        (0, "w"): [(A, KIND_W, 3)], (0, "d"): [(C, KIND_W, 2)],
        (0, "t0"): [(B, KIND_W, 3), (R1, 0)], (0, "t1"): [(R1, 1), (E, KIND_W, 1)],
        (1, "a0"): [(C, KIND_W, 3)],
        (1, "t0"): [(R1, 2), (E, KIND_W, 2)], (1, "t1"): [(R2, 0), (R1, 3)],
        (2, "a2"): [(R2, 1)], (2, "w"): [(R3, 0)],
        (2, "t0"): [(R1, 4)], (2, "t1"): [(R1, 5), (E, KIND_W, 3)],
        (3, "a0"): [(R3, 1)], (3, "a1"): [(R2, 2)], (3, "w"): [(R3, 2)], (3, "d"): [(R2, 3)],
        (3, "t0"): [(R1, 6)], (3, "t1"): [(R1, 7)],
    }

    @pl.loop(0, 4)
    def _(k):
        p = lax.rem(z + 4 - at_step(k), 4)

        def tick(name):
            ticks(k, {kk: steps for (kk, n), steps in FFN_TICKS.items() if n == name})

        def down_rows():
            return square(fd[p // 2, pl.ds(2 * lax.rem(p, 2), 2)])

        @pl.loop(0, tiles)
        def _(i):
            c = col(i)
            act, slope = gelu_both(nn(square(fw[p]), H1[:, c]))
            ZT[:, c] = act.astype(bf16)
            DU[:, c] = (nn(down_rows(), DM[:, c]) * slope).astype(bf16)
            for a in range(4):
                ticks(i * 8 + k, {a * 8 + kk: steps for (kk, n), steps in FFN_TICKS.items() if n == f"a{a}"})

        @pl.when(k > 0)
        def _():
            staged_free(2 * k - 2)
        stage_rows(0, lambda m: DU[m * 384:(m + 1) * 384, :], H1[...], True)
        to_sibling(2 * k)
        tick("w")

        @pl.when(k > 0)
        def _():
            staged_free(2 * k - 1)
        stage_rows(1, lambda m: ZT[m * 384:(m + 1) * 384, :], DM[...], False)
        to_sibling(2 * k + 1)
        tick("d")
        for half in range(2):
            c = slice(half * SLOTS, (half + 1) * SLOTS)
            MACC[:, c] += tn(down_rows(), ZT[:, c])
        tick("t0")
        for half in range(2):
            c = slice(half * SLOTS, (half + 1) * SLOTS)
            HACC[:, c] += tn(square(fw[p]), DU[:, c])
        tick("t1")

    move(spill_q, QKV, local.at[6])
    GG[...] = jnp.zeros_like(GG)

    @pl.loop(0, tiles)
    def _(i):
        c = col(i)
        v, m = X[:, c], MACC[:, c]
        MACC[:, c] = v + (m - jnp.mean(m, axis=0, keepdims=True))
        dx, part = norm_back(v, inv_rms(v), GCOL[1, :, :1], HACC[:, c])
        GG[...] += lane_fold(part)
        G[:, c] = G[:, c] + dx - dx[D - 1:, :]
        ticks(i, {0: [(R3, 3)], 2: [(R2, 4)]})
    GV[1] = jnp.sum(GG[...].T, axis=0, keepdims=True)

    @pl.when(s == 1)
    def _():
        move(MACC, out.at[:, mine], local.at[7])

    @pl.when(s == 0)
    def _():
        push(MACC, out.at[:, mine], i_s.at[5], i_r.at[5], sib)

    move(spill_x, HACC, local.at[5])

    @pl.loop(0, tiles)
    def _(i):
        c = col(i)
        v = G[:, c]
        DM[:, c] = (v - jnp.mean(v, axis=0, keepdims=True)).astype(bf16)

    staged_free(6)
    stage_rows(0, lambda m: DM[m * 384:(m + 1) * 384, :], ATT[...], True)
    to_sibling(8)
    R3(4)
    for half in range(2):
        c = slice(half * SLOTS, (half + 1) * SLOTS)
        H1[:, c] = tn(square(fa[3]), DM[:, c]).astype(bf16)
    R1(8)
    moved(spill_q, QKV, local.at[6])

    @pl.loop(0, 3 * nb)
    def _(i):
        b, spot = spots(i)
        scores, dprobs, probs, grads = {}, {}, {}, {}
        for u in units:
            head, off, c = spot(u)
            q, k, v = three(off, c)
            scores[u] = nn(k.T, q * bf16(SCALE))
            dprobs[u] = nn(v.T, H1[pl.ds(off, HEAD_DIM), c])
        for u in units:
            head, off, c = spot(u)
            p = jnp.exp(scores[u] + BIAS[b, u[1]] - LSE[pl.ds(head, 1), c])
            dp = dprobs[u]
            grads[u] = (p * (dp - jnp.sum(p * dp, axis=0, keepdims=True))).astype(bf16)
            probs[u] = p.astype(bf16)
        for u in units:
            head, off, c = spot(u)
            q, k, _ = three(off, c)
            QKV[pl.ds(off, HEAD_DIM), c] = (nn(k, grads[u]) * SCALE).astype(bf16)
            QKV[pl.ds(off + D, HEAD_DIM), c] = nt(q * bf16(SCALE), grads[u]).astype(bf16)
            QKV[pl.ds(off + 2 * D, HEAD_DIM), c] = nt(H1[pl.ds(off, HEAD_DIM), c], probs[u]).astype(bf16)
        ticks(i, {1: [(R2, 5)], 3: [(R3, 5)], 4: [(R2, 6)]})

    staged_free(7)
    stage_rows(1, lambda m: QKV[m * 384:(m + 1) * 384, :], H0[...], True)
    to_sibling(9)
    R3(6)
    R2(7)
    staged_free(8)
    stage_rows(0, lambda m: QKV[D + m * 384:D + (m + 1) * 384, :], H0[...], True)
    to_sibling(10)
    R1(9)
    staged_free(9)
    stage_rows(1, lambda m: QKV[2 * D + m * 384:2 * D + (m + 1) * 384, :], H0[...], True)
    to_sibling(11)
    R1(10)
    moved(spill_x, HACC, local.at[5])
    GG[...] = jnp.zeros_like(GG)

    @pl.loop(0, tiles)
    def _(i):
        c = col(i)
        v = HACC[:, c]
        dh = tn(square(fa[:3]), QKV[:, c])
        dx, part = norm_back(v, inv_rms(v), GCOL[0, :, :1], dh)
        GG[...] += lane_fold(part)
        G[:, c] = G[:, c] + dx - dx[D - 1:, :]
        ticks(i, {0: [(R1, 11)], 1: [(R3, 7)], 3: [(R2, 8)]})
    GV[0] = jnp.sum(GG[...].T, axis=0, keepdims=True)

    @pl.when(s == 0)
    def _():
        move(G, out.at[:, mine], local.at[8])

    @pl.when(s == 1)
    def _():
        push(G, out.at[:, mine], i_s.at[5], i_r.at[5], sib)

    push(GV.at[t], GL.at[0], gs.at[0], gr.at[0], sib)
    R3(8)
    R2(9)
    wait_recv(GL.at[0], gr.at[0])
    GT[0] = GV[s] + GL[0]
    push(GT.at[0], GL.at[1], gs.at[1], gr.at[1], n2)
    R3(9)
    R2(10)
    wait_recv(GL.at[1], gr.at[1])
    GT[1] = GT[0] + GL[1]
    push(GT.at[1], GL.at[2], gs.at[2], gr.at[2], n1)
    R3(10)
    R2(11)
    wait_recv(GL.at[2], gr.at[2])
    GT[2] = GT[1] + GL[2]
    for r in range(3):
        push(GT.at[2], GL.at[3 + r], gs.at[3 + r], gr.at[3 + r], at_plane(lax.rem(z + 1 + r, 4)))
    R3(11)

    def total_of(v, parts):
        v = wide(v)
        for part in parts:
            v = v + wide(part)
        return v

    for k in range(3):
        wait_recv(L3W.at[k], rw.at[k])
    FIN[1] = total_of(ACC[0, xy], [L3W[k] for k in range(3)])
    for sec in range(2):
        for r in range(3):
            zz = lax.rem(z + 1 + r, 4)
            wait_recv(L3D.at[sec, zz], rd.at[sec, zz])
        far = lax.rem(z + 4 - (2 * sec + z // 2), 4)
        FIND[sec] = total_of(ACC[2 * at_step(far) + 1, xy, lax.rem(z, 2)], [L3D[sec, lax.rem(z + 1 + r, 4)] for r in range(3)])
    move(FIND.at[s], down.at[s], local.at[9])
    push(FIND.at[t], down.at[s], i_s.at[6], i_r.at[6], sib)

    @pl.when(s == 1)
    def _():
        move(FIN.at[1], first.at[1], local.at[10])

    @pl.when(s == 0)
    def _():
        push(FIN.at[1], first.at[0], i_s.at[7], i_r.at[7], sib)

    for r in range(3):
        wait_recv(GL.at[3 + r], gr.at[3 + r])
    GT[3] = GT[2] + GL[3] + GL[4] + GL[5]
    gain_out[...] = GT[3]
    for r in range(3):
        zz = lax.rem(z + 1 + r, 4)
        wait_recv(L3A.at[zz], ra.at[zz])
    FIN[0] = total_of(ACC[8 + lax.rem(z + 1, 4), xy], [L3A[lax.rem(z + 1 + r, 4)] for r in range(3)])

    @pl.when(s == 0)
    def _():
        move(FIN.at[0], first.at[0], local.at[10])

    @pl.when(s == 1)
    def _():
        push(FIN.at[0], first.at[1], i_s.at[7], i_r.at[7], sib)

    @pl.when(s == 0)
    def _():
        moved(FIN.at[0], first.at[0], local.at[10])
        wait_send(FIN.at[1], i_s.at[7])
        wait_recv(first.at[1], i_r.at[7])
        wait_send(MACC, i_s.at[5])
        moved(G, out.at[:, mine], local.at[8])

    @pl.when(s == 1)
    def _():
        moved(FIN.at[1], first.at[1], local.at[10])
        wait_send(FIN.at[0], i_s.at[7])
        wait_recv(first.at[0], i_r.at[7])
        moved(MACC, out.at[:, mine], local.at[7])
        wait_send(G, i_s.at[5])

    wait_recv(out.at[:, other], i_r.at[5])
    moved(FIND.at[s], down.at[s], local.at[9])
    wait_send(FIND.at[t], i_s.at[6])
    wait_recv(down.at[t], i_r.at[6])
    wait_send(wd_ref.at[t], i_s.at[1])
    wait_send(gain_ref, i_s.at[2])
    a, b = rows_of(other)
    wait_send(a, i_s.at[3])
    wait_send(b, i_s.at[4])
    for n in range(6):
        wait_send(GT.at[0], gs.at[n])
    for kind in range(3):
        sent(kind)
    staged_free(10)
    staged_free(11)
    for j in range(SETS):
        scattered(j)


def finish_kernel(len_ref, pre, out, a, b, ins, outs):
    n = pre.shape[1] // SLOTS
    cols = lambda i: pl.ds(i * SLOTS, SLOTS)
    load = lambda i: pltpu.make_async_copy(pre.at[:, cols(i)], a.at[i % 2], ins.at[i % 2])
    save = lambda i: pltpu.make_async_copy(b.at[i % 2], out.at[:, 0, cols(i)], outs.at[i % 2])
    load(0).start()
    for i in range(n):
        load(i).wait()
        if i + 1 < n:
            load(i + 1).start()
        start, shift = 0, 0
        for j in range(4):
            shift = shift + jnp.where(len_ref[i, j] == LONGEST, start, 0)
            start = start + len_ref[i, j]
        if i >= 2:
            save(i - 2).wait()
        b[i % 2] = pltpu.roll(a[i % 2], shift, 1)[:D - 1]
        save(i).start()
    for i in range(max(n - 2, 0), n):
        save(i).wait()


def layer(lengths, mask, gain, stream, w, wd):
    T = stream.shape[2] // 2
    dma = lambda *shape: pltpu.SemaphoreType.DMA(shape)
    bulk = lambda *shape: pltpu.VMEM(shape, bf16)
    full = lambda *shape: pltpu.VMEM(shape, f32)
    scratch = [
        bulk(4, 4, 2, 96, D), bulk(4, 4, 2, 96, D), bulk(2, 4, 4, 2, 48, D),
        full(D, T), full(D, T), full(8, T), full(8, T),
        bulk(3 * D, T), bulk(D, T), bulk(D, T), bulk(D, T), bulk(D, T),
        full(D, T), full(D, T), full(T // SLOTS, 2, TILE, TILE), full(16, T), full(8, T),
        full(2, 1, D), full(2, D, 128), full(D, 128), full(2, 1, D), full(6, 1, D), full(4, 1, D),
        bulk(2, 4, 2, 2, 48, D), bulk(SETS, 4, 2, 48, D), bulk(SETS, 2, 2, 48, D), bulk(SETS, 2, 48, D),
        bulk(3, 2, 48, D), bulk(4, 2, 48, D), bulk(2, 4, 48, D), full(2, 2, 48, D), full(2, 48, D),
        dma(3, 4), dma(3, 4), dma(3, 4, 4), dma(3, 4, 4),
        dma(SETS), dma(SETS), dma(SETS, 2), dma(SETS, 2), dma(SETS), dma(SETS),
        dma(SETS, 2), dma(3), dma(4), dma(2, 4),
        dma(8), dma(8), dma(11), dma(6), dma(6),
    ]
    out, first, down, gains, _, _ = pl.pallas_call(
        layer_kernel,
        in_specs=[S, V, HBM, HBM, HBM, HBM],
        out_specs=[HBM, HBM, HBM, V, HBM, HBM],
        out_shape=[
            sds(D, 2 * T), sds(2, 2, 48, D), sds(2, 48, D), sds(1, D), sds(D, T), sds(3 * D, T, dtype=bf16),
        ],
        scratch_shapes=scratch,
        compiler_params=pltpu.CompilerParams(collective_id=1, has_side_effects=True, vmem_limit_bytes=VMEM_MOST),
        name="layer",
    )(lengths, mask, gain, stream, w.reshape(2, 96, D), wd.reshape(2, 48, D))
    final = pl.pallas_call(
        finish_kernel,
        in_specs=[S, HBM],
        out_specs=HBM,
        out_shape=sds(D - 1, 1, 2 * T),
        scratch_shapes=[full(2, D, SLOTS), full(2, D - 1, SLOTS), dma(2), dma(2)],
        compiler_params=pltpu.CompilerParams(vmem_limit_bytes=32 * 2**20),
        name="finish",
    )(lengths, out)
    return final, first.reshape(192, D), down.reshape(96, D), gains


def separate(own, stream, w, wd, gain, doc_lengths, pad_mask, sections, groups):
    s, d = own
    stream = jnp.pad(stream[:, 0], ((0, 1), (0, 0)))
    gain = jnp.broadcast_to(gain[0][:, None], (D, 128))
    T = stream.shape[1] // sections
    nb = T // SLOTS
    own_docs = lax.dynamic_slice_in_dim(doc_lengths, s * nb, nb, axis=0)
    ends = jnp.stack([jnp.sum(own_docs[:, : j + 1], axis=1) for j in range(own_docs.shape[1])], axis=1)
    mask = lax.dynamic_slice_in_dim(pad_mask, s * T, T, axis=0).astype(f32)
    mask = jnp.broadcast_to(mask[None], (8, T))
    weights = lax.all_gather(lax.all_gather(w, "dp", axis=0, tiled=True), "section")
    wd_full = lax.all_gather(wd, ("section", "dp"), axis=0, tiled=True)
    both = lax.all_gather(stream, "section")
    x, g = lax.dynamic_slice_in_dim(both, s * T, T, axis=2)
    gains = lax.all_gather(gain, "section")
    qkv, att, lse, h0, x1, h1 = run_attn_fwd(ends, x, gains[0], gains[1], mask, weights[0])
    out1, dy, gw1, gwd, gg1 = run_ffn(g, gains[1], mask, x1, h1, weights[1], wd_full)
    out0, gw0, gg0 = run_attn_bwd(ends, x, gains[0], mask, weights[0], qkv, att, lse, h0, dy)
    gw = jnp.stack([gw0, gw1])
    gg = jnp.stack([gg0, gg1])
    first = lax.psum_scatter(gw.astype(f32), "section", scatter_dimension=0)
    first = lax.psum_scatter(first, "dp", scatter_dimension=0, tiled=True)
    down = lax.psum_scatter(gwd.astype(f32), ("section", "dp"), scatter_dimension=0, tiled=True)
    outs = lax.all_gather(jnp.stack([out0, out1]), "section")
    out = jnp.concatenate([lax.dynamic_index_in_dim(outs[i], s, 0, False) for i in range(2)], axis=1)
    gain_total = lax.psum_scatter(lax.psum(jnp.sum(gg, axis=2), "dp"), "section", scatter_dimension=0)
    return out[: D - 1][:, None], first, down, gain_total[None]


def shards(sizes, stream_pair, norm_gains, first_proj, down_proj, doc_lengths, pad_mask):
    own = lax.axis_index("section"), lax.axis_index("dp")
    sections, groups = sizes
    stream = jnp.transpose(stream_pair, (2, 0, 1))
    w = jnp.transpose(first_proj[0])
    wd = jnp.transpose(down_proj)
    if sizes == (2, 16) and stream.shape[2] == 4 * SLOTS:
        out, first, down, gain_total = layer(doc_lengths, pad_mask[None], norm_gains, stream, w, wd)
    else:
        out, first, down, gain_total = separate(
            own, stream, w, wd, norm_gains, doc_lengths, pad_mask, sections, groups
        )
    share = D // groups
    gain_share = lax.dynamic_slice_in_dim(gain_total, own[1] * share, share, axis=1)
    return jnp.transpose(out, (1, 2, 0)), gain_share, jnp.transpose(first)[None], jnp.transpose(down)


def solution(mesh):
    placed = (
        P("section", "dp", None),
        P("section", None),
        P("section", None, "dp"),
        P(None, ("section", "dp")),
        P("dp", None),
        P("dp"),
    )
    return jax.shard_map(
        functools.partial(shards, (mesh.shape["section"], mesh.shape["dp"])),
        mesh=mesh,
        in_specs=placed,
        out_specs=(
            P("section", "dp", None),
            P("section", "dp"),
            P("section", None, "dp"),
            P(None, ("section", "dp")),
        ),
        check_vma=False,
    )
```

time: 510 us -> 204 us (0.40)
  Pallas kernels: 460 us -> 197 us
  local copies, waits for them, and re-layouts: 36.2 us -> 5.53 us
  other arithmetic: 12.7 us -> 0 us
    pallas_call x5 -> x2, Pallas kernels: 460 us -> 197 us  [the longest x1 191 us: layer(): pl.pallas_call(layer_kernel, in_specs=[S, V, HBM, HBM, HBM, HBM], out_spe...]
    unnamed x8 -> x10, local copies, waits for them, and re-layouts: 16.9 us -> 4.32 us
    another operation x2 -> x0, other arithmetic: 9.05 us -> none  [the longest x1 8.39 us: shards(): gw = jnp.stack([gw0, gw1])]
    slice x2 -> x0, local copies, waits for them, and re-layouts: 8.55 us -> none  [the longest x1 8.55 us: shards(): weights[1]]
where the time goes in v2:
time: 204 us; the launch traced here: 203 us
  Pallas kernels  197 us (97%)
  local copies, waits for them, and re-layouts  5.53 us (3%)
    pallas_call x1, Pallas kernels, layer(): pl.pallas_call(layer_kernel, in_specs=[S, V, HBM, HBM, HBM, HBM], out_spe...  191 us
    pallas_call x1, Pallas kernels, layer(): pl.pallas_call(finish_kernel, in_specs=[S, HBM], out_specs=HBM, out_shape...  5.19 us
    unnamed x10, local copies, waits for them, and re-layouts  4.32 us

profile of v2, /device:TPU:1, one launch (start us, length us, event | category | flops | bytes accessed | tf_op | source)
XLA Modules:
  0.0 202.8 jit_solution(2113765695906853024)
XLA Ops:
  0.6 0.0 copy-start.1
  0.6 191.4 %layer.1 = (f32[768,2048]{1,0:T(8,128)}, f32[2,2,48,768]{3,2,1,0:T(8,128)}, f32[2,48,768]{2,1,0:T(8,128)}, f32[1,768]{1,0:T(1,128)}, f32[768,1024]{1,0:T(8,128)}, /*index=5*/bf16[2304,1024]{1,0:T(8,128)(2,1)}) custom-call(s32[4,4]{1,0:T(4,128)} %len_ref.3, s32[1,2048]{1,0:T(1,128)} %bitcast.25, f32[1,768]{1,0:T(1,128)} %gain_ref.1, ...), custom_call_target="tpu_custom_call" | custom-call | tf_op jit(solution)/shard_map/layer/pallas_call | solution.py:959
  192.1 0.0 copy-done.1
  192.1 0.0 copy-start
  192.1 2.8 %copy-done = f32[768,2048]{1,0:T(8,128)S(1)} copy-done((f32[768,2048]{1,0:T(8,128)S(1)}, f32[768,2048]{1,0:T(8,128)}, u32[]{:S(2)}) %copy-start) | copy-done | bytes 6291480
  194.9 0.0 copy-start.2
  194.9 0.0 copy-start.3
  194.9 5.2 %finish.1 = f32[767,1,2048]{2,1,0:T(1,128)} custom-call(s32[4,4]{1,0:T(4,128)S(1)} %copy-done.1, f32[768,2048]{1,0:T(8,128)S(1)} %copy-done), custom_call_target="tpu_custom_call" | custom-call | tf_op jit(solution)/shard_map/finish/pallas_call | solution.py:970
  200.1 1.2 constant_dynamic-slice_fusion
  201.3 0.0 copy-done.2
  201.3 0.8 copy.12
  202.1 0.0 copy-done.3
  202.1 0.7 copy.13
Async XLA Ops:
  0.6 191.5 %copy-start.1 = (s32[4,4]{1,0:T(4,128)S(1)}, s32[4,4]{1,0:T(4,128)}, u32[]{:S(2)}) copy-start(s32[4,4]{1,0:T(4,128)} %len_ref.3) | copy-start | bytes 196
  192.1 2.8 %copy-start = (f32[768,2048]{1,0:T(8,128)S(1)}, f32[768,2048]{1,0:T(8,128)}, u32[]{:S(2)}) copy-start(f32[768,2048]{1,0:T(8,128)} %get-tuple-element.8.pre) | copy-start | bytes 18874372
  194.9 6.4 %copy-start.2 = (f32[2,2,48,768]{3,2,1,0:T(8,128)S(1)}, f32[2,2,48,768]{3,2,1,0:T(8,128)}, u32[]{:S(2)}) copy-start(f32[2,2,48,768]{3,2,1,0:T(8,128)} %get-tuple-element.10) | copy-start | bytes 1769476
  194.9 7.2 %copy-start.3 = (f32[2,48,768]{2,1,0:T(8,128)S(1)}, f32[2,48,768]{2,1,0:T(8,128)}, u32[]{:S(2)}) copy-start(f32[2,48,768]{2,1,0:T(8,128)} %get-tuple-element.11) | copy-start | bytes 884740

commit v3 on v2

--- a/solution.py
+++ b/solution.py
@@ -245,6 +245,7 @@
 
 
 DIST = (0, 1, 3, 2)
+CHUNKS = (0, 2, 1, 3)
 TILE = 256
 SCALE = HEAD_DIM ** -0.5
 KIND_A, KIND_D, KIND_W = 0, 1, 2
@@ -261,15 +262,15 @@
 
 
 def at_step(k):
-    return (1 - k // 2) * k + (k // 2) * (5 - k)
+    return lax.rem(2 * k, 3) + 3 * (k // 3)
 
 
 def layer_kernel(
     len_ref, mask_ref, gain_ref, stream, w_ref, wd_ref,
     out, first, down, gain_out, spill_x, spill_q,
     fa, fw, fd, X, G, xt, gt, QKV, ATT, H0, H1, DM, MACC, HACC, BIAS, LSE, MK, GR, GCOL, GG, GV, GL, GT,
-    STG, ACC, L1, L2, L3W, L3A, L3D, FIN, FIND,
-    zs, zr, ps, pr, ss, sr, p1s, p1r, p2s, p2r, p3s, rw, ra, rd, i_s, i_r, local, gs, gr,
+    STG, STGD, ACC, L1, L2, L3W, L3A, L3D,
+    zs, zr, ps, pr, ss, sr, p1s, p1r, p2s, p2r, p3s, rw, ra, rd, i_s, i_r, local, gs, gr, gss, gsr,
 ):
     s, d = lax.axis_index("section"), lax.axis_index("dp")
     x, y, z, xy = lax.rem(d, 2), lax.rem(d // 2, 2), d // 4, lax.rem(d, 4)
@@ -283,8 +284,10 @@
     col = lambda i: pl.ds(pl.multiple_of(i * TILE, TILE), TILE)
     at_plane = lambda p: (s, p * 4 + xy)
 
-    def plane(i):
-        return lax.rem(z + 4 - DIST[i], 4)
+    def plane(i, kind=KIND_W):
+        if kind == KIND_D:
+            return 2 * lax.rem(z + i // 2, 2) + i % 2
+        return lax.rem(z + 4 - (DIST if kind == KIND_A else CHUNKS)[i], 4)
 
     def wait_recv(dst, sem):
         pltpu.make_async_remote_copy(
@@ -308,39 +311,50 @@
     def group(kind, zz, h):
         return fd.at[:, zz, :, h] if kind == KIND_D else (fa, None, fw)[kind].at[zz, :, h]
 
-    def Z(kind, i):
+    def Z(kind, far):
         own = slab(kind, z, xy, s)
-        push(own, own, zs.at[kind, i], zr.at[kind, i], at_plane(lax.rem(z + DIST[i], 4)))
+        push(own, own, zs.at[kind, far], zr.at[kind, far], at_plane(lax.rem(z + far, 4)))
 
     def A(kind, i):
-        here = slab(kind, plane(i), xy, s)
-        if i:
-            wait_recv(here, zr.at[kind, i])
-        if 0 < i < 3:
-            Z(kind, i + 1)
-        elif i == 3 and kind < 2:
-            Z(kind + 1, 1)
+        zz = plane(i, kind)
+        here = slab(kind, zz, xy, s)
+        if kind == KIND_D:
+            @pl.when(zz != z)
+            def _():
+                wait_recv(here, zr.at[kind, lax.rem(z + 4 - zz, 4)])
+        elif i:
+            wait_recv(here, zr.at[kind, (DIST if kind == KIND_A else CHUNKS)[i]])
+        if kind == KIND_A and i in (1, 2):
+            Z(kind, DIST[i + 1])
+        elif kind == KIND_A and i == 3:
+            for far in (1, 2, 3):
+                Z(KIND_D, far)
+        elif kind == KIND_D and i == 1:
+            Z(KIND_W, 2)
+        elif kind == KIND_W and i == 1:
+            Z(KIND_W, 1)
+            Z(KIND_W, 3)
         push(here, here, ps.at[kind, i, 0], pr.at[kind, i, 0], n1)
         push(here, here, ps.at[kind, i, 1], pr.at[kind, i, 1], n2)
 
     def B(kind, i):
-        here = slab(kind, plane(i), xy1, s)
+        here = slab(kind, plane(i, kind), xy1, s)
         wait_recv(here, pr.at[kind, i, 0])
         push(here, here, ps.at[kind, i, 2], pr.at[kind, i, 2], n2)
 
     def C(kind, i):
-        zz = plane(i)
+        zz = plane(i, kind)
         wait_recv(slab(kind, zz, xy2, s), pr.at[kind, i, 1])
         wait_recv(slab(kind, zz, xy3, s), pr.at[kind, i, 2])
         here = group(kind, zz, s)
         push(here, here, ps.at[kind, i, 3], pr.at[kind, i, 3], sib)
 
     def E(kind, i):
-        wait_recv(group(kind, plane(i), t), pr.at[kind, i, 3])
+        wait_recv(group(kind, plane(i, kind), t), pr.at[kind, i, 3])
 
     def sent(kind):
         for i in range(4):
-            zz = plane(i)
+            zz = plane(i, kind)
             if i:
                 wait_send(slab(kind, z, xy, s), zs.at[kind, i])
             wait_send(slab(kind, zz, xy, s), ps.at[kind, i, 0])
@@ -348,16 +362,33 @@
             wait_send(slab(kind, zz, xy1, s), ps.at[kind, i, 2])
             wait_send(group(kind, zz, s), ps.at[kind, i, 3])
 
-    def to_sibling(j):
-        push(STG.at[j % 2 if isinstance(j, int) else lax.rem(j, 2), :, t], ACC.at[j], ss.at[j], sr.at[j], sib)
-
-    def staged_free(j):
-        wait_send(STG.at[0, :, t], ss.at[j])
+    def to_sibling(j, slot, down_set=False):
+        if down_set:
+            for sub in range(2):
+                push(STGD.at[sub, :, t], ACC.at[j, :, sub], ss.at[j, sub], sr.at[j, sub], sib)
+        else:
+            push(STG.at[slot, :, t], ACC.at[j], ss.at[j, 0], sr.at[j, 0], sib)
+
+    def staged_free(j, down_set=False):
+        if down_set:
+            for sub in range(2):
+                wait_send(STGD.at[sub, :, t], ss.at[j, sub])
+        else:
+            wait_send(STG.at[0, :, t], ss.at[j, 0])
+
+    def slot_of(j):
+        return j // 2 % 2 if j < 8 else j % 2
 
     def R1(j):
-        wait_recv(ACC.at[j], sr.at[j])
-        for q in range(4):
-            ACC[j, q] = (wide(ACC[j, q]) + wide(STG[j % 2, q, s])).astype(bf16)
+        if j < 8 and j % 2:
+            for sub in range(2):
+                wait_recv(ACC.at[j, :, sub], sr.at[j, sub])
+                for q in range(4):
+                    ACC[j, q, sub] = (wide(ACC[j, q, sub]) + wide(STGD[sub, q, s])).astype(bf16)
+        else:
+            wait_recv(ACC.at[j], sr.at[j, 0])
+            for q in range(4):
+                ACC[j, q] = (wide(ACC[j, q]) + wide(STG[slot_of(j), q, s])).astype(bf16)
         push(ACC.at[j, xy2], L1.at[j, 0], p1s.at[j, 0], p1r.at[j, 0], n2)
         push(ACC.at[j, xy3], L1.at[j, 1], p1s.at[j, 1], p1r.at[j, 1], n2)
 
@@ -398,6 +429,43 @@
         for cond, src, dst, ssem, rsem, to in ends_of(j):
             guarded(cond, lambda src=src, ssem=ssem: wait_send(src, ssem))
 
+    QKV_SETS = pl.ds(9, 3)
+
+    def G1(n):
+        q = (lax.rem(y + 1 - n % 2, 2)) * 2 + lax.rem(x + 1 - n // 2, 2)
+        slot = (n + 1) % 2
+        wait_recv(ACC.at[QKV_SETS, q], gsr.at[n])
+        for part in range(3):
+            ACC[9 + part, q] = (wide(ACC[9 + part, q]) + wide(STG[slot, part, s])).astype(bf16)
+        if n == 0:
+            push(ACC.at[QKV_SETS, xy3], L1.at[QKV_SETS, 1], p1s.at[9, 1], p1r.at[9, 1], n2)
+        elif n < 3:
+            @pl.when(s == n - 1)
+            def _():
+                push(ACC.at[QKV_SETS, xy2], L1.at[QKV_SETS, 0], p1s.at[9, 0], p1r.at[9, 0], n2)
+
+    def G2():
+        wait_recv(L1.at[QKV_SETS, 1], p1r.at[9, 1])
+        for j in range(9, 12):
+            ACC[j, xy1] = (wide(ACC[j, xy1]) + wide(L1[j, 1])).astype(bf16)
+        push(ACC.at[QKV_SETS, xy1], L2.at[QKV_SETS], p2s.at[9], p2r.at[9], n1)
+
+    def G3():
+        wait_recv(L1.at[QKV_SETS, 0], p1r.at[9, 0])
+        wait_recv(L2.at[QKV_SETS], p2r.at[9])
+        for j in range(9, 12):
+            ACC[j, xy] = (wide(ACC[j, xy]) + wide(L1[j, 0]) + wide(L2[j])).astype(bf16)
+            for cond, src, dst, ssem, rsem, to in ends_of(j):
+                guarded(cond, lambda src=src, dst=dst, ssem=ssem, rsem=rsem, to=to: push(src, dst, ssem, rsem, at_plane(to)) and None)
+
+    def G_sent():
+        wait_send(ACC.at[QKV_SETS, xy3], p1s.at[9, 1])
+        wait_send(ACC.at[QKV_SETS, xy2], p1s.at[9, 0])
+        wait_send(ACC.at[QKV_SETS, xy1], p2s.at[9])
+        for j in range(9, 12):
+            for cond, src, dst, ssem, rsem, to in ends_of(j):
+                guarded(cond, lambda src=src, ssem=ssem: wait_send(src, ssem))
+
     barrier = pltpu.get_barrier_semaphore()
     partners = [sib, n1, n2, *(at_plane(lax.rem(z + r, 4)) for r in (1, 2, 3))]
     for device in partners:
@@ -451,7 +519,7 @@
     def _():
         wait_recv(fa.at[z, xy, 1], i_r.at[0])
 
-    Z(KIND_A, 1)
+    Z(KIND_A, DIST[1])
     A(KIND_A, 0)
     pl.when(s == 0)(stream_out(X, xt))
     pl.when(s == 1)(stream_out(G, gt))
@@ -545,16 +613,16 @@
             DM[:, c] = (v - jnp.mean(v, axis=0, keepdims=True)).astype(bf16)
 
     masks()
+    A(KIND_A, 1)
     B(KIND_A, 0)
     x_arrived()
     turn(X, xt, 0)
-    A(KIND_A, 1)
+    A(KIND_A, 2)
+    B(KIND_A, 1)
     turn(X, xt, 1)
     C(KIND_A, 0)
     normed_in()
     move(X, spill_x, local.at[5])
-    B(KIND_A, 1)
-    A(KIND_A, 2)
 
     @pl.when(s == 0)
     def _():
@@ -567,19 +635,21 @@
 
     moved(wd_ref.at[s], fd.at[s, z, xy, s], local.at[1])
     wait_recv(fd.at[t, z, xy, s], i_r.at[1])
-    C(KIND_A, 1)
+    A(KIND_A, 3)
     B(KIND_A, 2)
     g_arrived()
     turn(G, gt, 0)
-    A(KIND_A, 3)
+    C(KIND_A, 1)
+    A(KIND_D, 0)
+    B(KIND_A, 3)
     turn(G, gt, 1)
     C(KIND_A, 2)
     cotangent()
-    B(KIND_A, 3)
-    A(KIND_D, 0)
     C(KIND_A, 3)
     for i in range(4):
         E(KIND_A, i)
+    A(KIND_D, 1)
+    B(KIND_D, 0)
 
     def ticks(index, table):
         for at, steps in table.items():
@@ -592,7 +662,7 @@
     def _(p):
         rows = pl.ds(pl.multiple_of(p * D, D), D)
         QKV[rows, :] = nn(square(fa[p]), H0[...]).astype(bf16)
-        ticks(p, {0: [(B, KIND_D, 0)], 2: [(A, KIND_D, 1)]})
+        ticks(p, {1: [(A, KIND_W, 0), (B, KIND_D, 1)], 2: [(C, KIND_D, 0)]})
 
     units = [(h, qb) for h in range(4) for qb in range(2)]
 
@@ -625,7 +695,7 @@
         for u in units:
             head, off, c = spot(u)
             ATT[pl.ds(off, HEAD_DIM), c] = nn(QKV[pl.ds(off + 2 * D, HEAD_DIM), c], probs[u]).astype(bf16)
-        ticks(i, {0: [(C, KIND_D, 0)], 1: [(B, KIND_D, 1)], 3: [(A, KIND_D, 2), (C, KIND_D, 1)], 5: [(B, KIND_D, 2)]})
+        ticks(i, {1: [(A, KIND_W, 1), (B, KIND_W, 0), (C, KIND_D, 1)], 3: [(A, KIND_D, 2), (B, KIND_W, 1)], 5: [(C, KIND_W, 0)]})
 
     move(QKV, spill_q, local.at[6])
     moved(X, spill_x, local.at[5])
@@ -638,46 +708,34 @@
         v = expanded(jnp.where(last_row(v.shape), 0.0, v))
         X[:, c] = v
         H1[:, c] = (v * inv_rms(v) * GCOL[1, :, :1]).astype(bf16)
-        ticks(i, {1: [(A, KIND_D, 3)], 2: [(C, KIND_D, 2)], 3: [(B, KIND_D, 3)]})
+        ticks(i, {0: [(A, KIND_D, 3), (B, KIND_D, 2)], 2: [(C, KIND_W, 1)]})
 
     MACC[...] = jnp.zeros_like(MACC)
     HACC[...] = jnp.zeros_like(HACC)
     moved(QKV, spill_q, local.at[6])
-    A(KIND_W, 0)
-    C(KIND_D, 3)
-    for i in range(4):
-        E(KIND_D, i)
-    B(KIND_W, 0)
-    A(KIND_W, 1)
-    C(KIND_W, 0)
-    B(KIND_W, 1)
+    A(KIND_W, 2)
+    B(KIND_D, 3)
+    E(KIND_D, 0)
+    E(KIND_D, 1)
     E(KIND_W, 0)
     ZT, DU = QKV.at[pl.ds(0, D)], QKV.at[pl.ds(D, D)]
 
     def stage_rows(slot, left, right, by_plane):
-        for m in range(2):
-            v = nt(left(m), right).astype(bf16)
-            if by_plane:
-                for a in range(2):
-                    for h in range(2):
-                        for sub in range(2):
-                            lo = a * 192 + h * 96 + sub * 48
-                            STG[slot, 2 * m + a, h, sub] = v[lo:lo + 48]
-            else:
-                for q in range(4):
-                    for h in range(2):
-                        STG[slot, q, h, m] = v[q * 96 + h * 48:q * 96 + h * 48 + 48]
+        v = nt(left, right).astype(bf16)
+        if by_plane:
+            STG[slot] = v.reshape(4, 2, 2, 48, D)
+        else:
+            STGD[...] = v.reshape(2, 4, 2, 48, D)
 
     FFN_TICKS = {
-        (0, "a1"): [(A, KIND_W, 2)], (0, "a2"): [(C, KIND_W, 1)], (0, "a3"): [(B, KIND_W, 2)],
-        (0, "w"): [(A, KIND_W, 3)], (0, "d"): [(C, KIND_W, 2)],
-        (0, "t0"): [(B, KIND_W, 3), (R1, 0)], (0, "t1"): [(R1, 1), (E, KIND_W, 1)],
-        (1, "a0"): [(C, KIND_W, 3)],
-        (1, "t0"): [(R1, 2), (E, KIND_W, 2)], (1, "t1"): [(R2, 0), (R1, 3)],
-        (2, "a2"): [(R2, 1)], (2, "w"): [(R3, 0)],
-        (2, "t0"): [(R1, 4)], (2, "t1"): [(R1, 5), (E, KIND_W, 3)],
-        (3, "a0"): [(R3, 1)], (3, "a1"): [(R2, 2)], (3, "w"): [(R3, 2)], (3, "d"): [(R2, 3)],
-        (3, "t0"): [(R1, 6)], (3, "t1"): [(R1, 7)],
+        (0, "a"): [(A, KIND_W, 3), (B, KIND_W, 2), (C, KIND_D, 2)],
+        (0, "w"): [(C, KIND_D, 3)], (0, "d"): [(B, KIND_W, 3), (C, KIND_W, 2)],
+        (0, "t0"): [(R1, 0)], (0, "t1"): [(R1, 1), (E, KIND_W, 1)],
+        (1, "a"): [(C, KIND_W, 3)], (1, "t0"): [(R1, 2)],
+        (1, "t1"): [(R1, 3), (R2, 0), (E, KIND_D, 2), (E, KIND_D, 3), (E, KIND_W, 2)],
+        (2, "a"): [(R2, 1)], (2, "d"): [(R3, 0)], (2, "t0"): [(R1, 4), (R2, 2)],
+        (2, "t1"): [(R1, 5), (R3, 1), (E, KIND_W, 3)],
+        (3, "a"): [(R2, 3)], (3, "d"): [(R3, 2)], (3, "t0"): [(R1, 6), (R2, 4)], (3, "t1"): [(R1, 7), (R3, 3)],
     }
 
     @pl.loop(0, 4)
@@ -690,35 +748,31 @@
         def down_rows():
             return square(fd[p // 2, pl.ds(2 * lax.rem(p, 2), 2)])
 
-        @pl.loop(0, tiles)
-        def _(i):
-            c = col(i)
+        for i in range(tiles):
+            c = slice(i * TILE, (i + 1) * TILE)
             act, slope = gelu_both(nn(square(fw[p]), H1[:, c]))
             ZT[:, c] = act.astype(bf16)
             DU[:, c] = (nn(down_rows(), DM[:, c]) * slope).astype(bf16)
-            for a in range(4):
-                ticks(i * 8 + k, {a * 8 + kk: steps for (kk, n), steps in FFN_TICKS.items() if n == f"a{a}"})
+        tick("a")
+
+        slot = lax.rem(k, 2)
+
+        @pl.when(k > 1)
+        def _():
+            staged_free(2 * k - 4)
+        stage_rows(slot, DU[...], H1[...], True)
+        to_sibling(2 * k, slot)
+        tick("w")
 
         @pl.when(k > 0)
         def _():
-            staged_free(2 * k - 2)
-        stage_rows(0, lambda m: DU[m * 384:(m + 1) * 384, :], H1[...], True)
-        to_sibling(2 * k)
-        tick("w")
-
-        @pl.when(k > 0)
-        def _():
-            staged_free(2 * k - 1)
-        stage_rows(1, lambda m: ZT[m * 384:(m + 1) * 384, :], DM[...], False)
-        to_sibling(2 * k + 1)
+            staged_free(2 * k - 1, True)
+        stage_rows(0, ZT[...], DM[...], False)
+        to_sibling(2 * k + 1, 0, True)
         tick("d")
-        for half in range(2):
-            c = slice(half * SLOTS, (half + 1) * SLOTS)
-            MACC[:, c] += tn(down_rows(), ZT[:, c])
+        MACC[...] += tn(down_rows(), ZT[...])
         tick("t0")
-        for half in range(2):
-            c = slice(half * SLOTS, (half + 1) * SLOTS)
-            HACC[:, c] += tn(square(fw[p]), DU[:, c])
+        HACC[...] += tn(square(fw[p]), DU[...])
         tick("t1")
 
     move(spill_q, QKV, local.at[6])
@@ -732,7 +786,7 @@
         dx, part = norm_back(v, inv_rms(v), GCOL[1, :, :1], HACC[:, c])
         GG[...] += lane_fold(part)
         G[:, c] = G[:, c] + dx - dx[D - 1:, :]
-        ticks(i, {0: [(R3, 3)], 2: [(R2, 4)]})
+        ticks(i, {2: [(R2, 5)]})
     GV[1] = jnp.sum(GG[...].T, axis=0, keepdims=True)
 
     @pl.when(s == 1)
@@ -751,64 +805,88 @@
         v = G[:, c]
         DM[:, c] = (v - jnp.mean(v, axis=0, keepdims=True)).astype(bf16)
 
+    staged_free(4)
     staged_free(6)
-    stage_rows(0, lambda m: DM[m * 384:(m + 1) * 384, :], ATT[...], True)
-    to_sibling(8)
-    R3(4)
-    for half in range(2):
-        c = slice(half * SLOTS, (half + 1) * SLOTS)
-        H1[:, c] = tn(square(fa[3]), DM[:, c]).astype(bf16)
+    staged_free(7, True)
+    stage_rows(0, DM[...], ATT[...], True)
+    to_sibling(8, 0)
+    H1[...] = tn(square(fa[3]), DM[...]).astype(bf16)
     R1(8)
     moved(spill_q, QKV, local.at[6])
 
-    @pl.loop(0, 3 * nb)
-    def _(i):
-        b, spot = spots(i)
-        scores, dprobs, probs, grads = {}, {}, {}, {}
-        for u in units:
-            head, off, c = spot(u)
-            q, k, v = three(off, c)
-            scores[u] = nn(k.T, q * bf16(SCALE))
-            dprobs[u] = nn(v.T, H1[pl.ds(off, HEAD_DIM), c])
-        for u in units:
-            head, off, c = spot(u)
-            p = jnp.exp(scores[u] + BIAS[b, u[1]] - LSE[pl.ds(head, 1), c])
-            dp = dprobs[u]
-            grads[u] = (p * (dp - jnp.sum(p * dp, axis=0, keepdims=True))).astype(bf16)
-            probs[u] = p.astype(bf16)
-        for u in units:
-            head, off, c = spot(u)
-            q, k, _ = three(off, c)
-            QKV[pl.ds(off, HEAD_DIM), c] = (nn(k, grads[u]) * SCALE).astype(bf16)
-            QKV[pl.ds(off + D, HEAD_DIM), c] = nt(q * bf16(SCALE), grads[u]).astype(bf16)
-            QKV[pl.ds(off + 2 * D, HEAD_DIM), c] = nt(H1[pl.ds(off, HEAD_DIM), c], probs[u]).astype(bf16)
-        ticks(i, {1: [(R2, 5)], 3: [(R3, 5)], 4: [(R2, 6)]})
-
-    staged_free(7)
-    stage_rows(1, lambda m: QKV[m * 384:(m + 1) * 384, :], H0[...], True)
-    to_sibling(9)
-    R3(6)
-    R2(7)
-    staged_free(8)
-    stage_rows(0, lambda m: QKV[D + m * 384:D + (m + 1) * 384, :], H0[...], True)
-    to_sibling(10)
-    R1(9)
-    staged_free(9)
-    stage_rows(1, lambda m: QKV[2 * D + m * 384:2 * D + (m + 1) * 384, :], H0[...], True)
-    to_sibling(11)
-    R1(10)
+    GROUP_TICKS = {
+        (0, "0"): [(R3, 4)], (0, "1"): [(R2, 6)], (0, "g"): [(R3, 5)],
+        (1, "0"): [(R2, 7), (G1, 0)], (1, "1"): [(R3, 6)], (1, "g"): [(R2, 8)],
+        (2, "0"): [(R3, 7), (G1, 1)], (2, "g"): [(R3, 8)],
+        (3, "0"): [(G1, 2), (G2,)],
+    }
+
+    @pl.loop(0, 4)
+    def _(n):
+        q = lax.rem(y + 1 - lax.rem(n, 2), 2) * 2 + lax.rem(x + 1 - n // 2, 2)
+
+        def tick(name):
+            ticks(n, {nn_: steps for (nn_, name_), steps in GROUP_TICKS.items() if name_ == name})
+
+        for b in range(nb):
+            picks = [(h, qb) for h in range(3) for qb in range(2)]
+            spot = lambda u: (q * 3 + u[0], pl.multiple_of((q * 3 + u[0]) * HEAD_DIM, HEAD_DIM), slice(b * SLOTS + u[1] * TILE, b * SLOTS + (u[1] + 1) * TILE))
+            scores, dprobs, probs, grads = {}, {}, {}, {}
+            for u in picks:
+                head, off, c = spot(u)
+                qq, kk, vv = three(off, c)
+                scores[u] = nn(kk.T, qq * bf16(SCALE))
+                dprobs[u] = nn(vv.T, H1[pl.ds(off, HEAD_DIM), c])
+            for u in picks:
+                head, off, c = spot(u)
+                p = jnp.exp(scores[u] + BIAS[b, u[1]] - LSE[pl.ds(head, 1), c])
+                dp = dprobs[u]
+                grads[u] = (p * (dp - jnp.sum(p * dp, axis=0, keepdims=True))).astype(bf16)
+                probs[u] = p.astype(bf16)
+            for u in picks:
+                head, off, c = spot(u)
+                qq, kk, _ = three(off, c)
+                QKV[pl.ds(off, HEAD_DIM), c] = (nn(kk, grads[u]) * SCALE).astype(bf16)
+                QKV[pl.ds(off + D, HEAD_DIM), c] = nt(qq * bf16(SCALE), grads[u]).astype(bf16)
+                QKV[pl.ds(off + 2 * D, HEAD_DIM), c] = nt(H1[pl.ds(off, HEAD_DIM), c], probs[u]).astype(bf16)
+            tick(str(b))
+        slot = lax.rem(n + 1, 2)
+
+        @pl.when(n == 1)
+        def _():
+            staged_free(8)
+
+        @pl.when(n > 1)
+        def _():
+            wait_send(STG.at[0, pl.ds(0, 3), t], gss.at[n - 2])
+        rows = lambda part: QKV[pl.ds(pl.multiple_of(part * D + q * 192, 64), 192), :]
+        v = nt(jnp.concatenate([rows(0), rows(1), rows(2)], axis=0), H0[...]).astype(bf16)
+        STG[slot, 0:3] = v.reshape(3, 2, 2, 48, D)
+        push(STG.at[slot, pl.ds(0, 3), t], ACC.at[QKV_SETS, q], gss.at[n], gsr.at[n], sib)
+        tick("g")
+
     moved(spill_x, HACC, local.at[5])
+
+    @pl.when(s == 1)
+    def _():
+        moved(MACC, out.at[:, mine], local.at[7])
+
+    @pl.when(s == 0)
+    def _():
+        wait_send(MACC, i_s.at[5])
+
+    G1(3)
+    MACC[...] = tn(square(fa[:3]), QKV[...])
+    G3()
     GG[...] = jnp.zeros_like(GG)
 
     @pl.loop(0, tiles)
     def _(i):
         c = col(i)
         v = HACC[:, c]
-        dh = tn(square(fa[:3]), QKV[:, c])
-        dx, part = norm_back(v, inv_rms(v), GCOL[0, :, :1], dh)
+        dx, part = norm_back(v, inv_rms(v), GCOL[0, :, :1], MACC[:, c])
         GG[...] += lane_fold(part)
         G[:, c] = G[:, c] + dx - dx[D - 1:, :]
-        ticks(i, {0: [(R1, 11)], 1: [(R3, 7)], 3: [(R2, 8)]})
     GV[0] = jnp.sum(GG[...].T, axis=0, keepdims=True)
 
     @pl.when(s == 0)
@@ -820,49 +898,45 @@
         push(G, out.at[:, mine], i_s.at[5], i_r.at[5], sib)
 
     push(GV.at[t], GL.at[0], gs.at[0], gr.at[0], sib)
-    R3(8)
-    R2(9)
     wait_recv(GL.at[0], gr.at[0])
     GT[0] = GV[s] + GL[0]
     push(GT.at[0], GL.at[1], gs.at[1], gr.at[1], n2)
-    R3(9)
-    R2(10)
     wait_recv(GL.at[1], gr.at[1])
     GT[1] = GT[0] + GL[1]
     push(GT.at[1], GL.at[2], gs.at[2], gr.at[2], n1)
-    R3(10)
-    R2(11)
     wait_recv(GL.at[2], gr.at[2])
     GT[2] = GT[1] + GL[2]
     for r in range(3):
         push(GT.at[2], GL.at[3 + r], gs.at[3 + r], gr.at[3 + r], at_plane(lax.rem(z + 1 + r, 4)))
-    R3(11)
 
     def total_of(v, parts):
         v = wide(v)
         for part in parts:
             v = v + wide(part)
-        return v
+        return square(v)
+
+    whole = lambda i: HACC.at[pl.ds(i * 96, 96), pl.ds(0, D)]
+    lower = lambda i: HACC.at[pl.ds(pl.multiple_of(192 + 48 * i, 16), 48), pl.ds(0, D)]
 
     for k in range(3):
         wait_recv(L3W.at[k], rw.at[k])
-    FIN[1] = total_of(ACC[0, xy], [L3W[k] for k in range(3)])
+    whole(1)[...] = total_of(ACC[0, xy], [L3W[k] for k in range(3)])
     for sec in range(2):
         for r in range(3):
             zz = lax.rem(z + 1 + r, 4)
             wait_recv(L3D.at[sec, zz], rd.at[sec, zz])
         far = lax.rem(z + 4 - (2 * sec + z // 2), 4)
-        FIND[sec] = total_of(ACC[2 * at_step(far) + 1, xy, lax.rem(z, 2)], [L3D[sec, lax.rem(z + 1 + r, 4)] for r in range(3)])
-    move(FIND.at[s], down.at[s], local.at[9])
-    push(FIND.at[t], down.at[s], i_s.at[6], i_r.at[6], sib)
+        lower(sec)[...] = total_of(ACC[2 * at_step(far) + 1, xy, lax.rem(z, 2)], [L3D[sec, lax.rem(z + 1 + r, 4)] for r in range(3)])
+    move(lower(s), down.at[s], local.at[9])
+    push(lower(t), down.at[s], i_s.at[6], i_r.at[6], sib)
 
     @pl.when(s == 1)
     def _():
-        move(FIN.at[1], first.at[1], local.at[10])
+        move(whole(1), first.at[1], local.at[10])
 
     @pl.when(s == 0)
     def _():
-        push(FIN.at[1], first.at[0], i_s.at[7], i_r.at[7], sib)
+        push(whole(1), first.at[0], i_s.at[7], i_r.at[7], sib)
 
     for r in range(3):
         wait_recv(GL.at[3 + r], gr.at[3 + r])
@@ -871,35 +945,33 @@
     for r in range(3):
         zz = lax.rem(z + 1 + r, 4)
         wait_recv(L3A.at[zz], ra.at[zz])
-    FIN[0] = total_of(ACC[8 + lax.rem(z + 1, 4), xy], [L3A[lax.rem(z + 1 + r, 4)] for r in range(3)])
+    whole(0)[...] = total_of(ACC[8 + lax.rem(z + 1, 4), xy], [L3A[lax.rem(z + 1 + r, 4)] for r in range(3)])
 
     @pl.when(s == 0)
     def _():
-        move(FIN.at[0], first.at[0], local.at[10])
+        move(whole(0), first.at[0], local.at[10])
 
     @pl.when(s == 1)
     def _():
-        push(FIN.at[0], first.at[1], i_s.at[7], i_r.at[7], sib)
+        push(whole(0), first.at[1], i_s.at[7], i_r.at[7], sib)
 
     @pl.when(s == 0)
     def _():
-        moved(FIN.at[0], first.at[0], local.at[10])
-        wait_send(FIN.at[1], i_s.at[7])
+        moved(whole(0), first.at[0], local.at[10])
+        wait_send(whole(1), i_s.at[7])
         wait_recv(first.at[1], i_r.at[7])
-        wait_send(MACC, i_s.at[5])
         moved(G, out.at[:, mine], local.at[8])
 
     @pl.when(s == 1)
     def _():
-        moved(FIN.at[1], first.at[1], local.at[10])
-        wait_send(FIN.at[0], i_s.at[7])
+        moved(whole(1), first.at[1], local.at[10])
+        wait_send(whole(0), i_s.at[7])
         wait_recv(first.at[0], i_r.at[7])
-        moved(MACC, out.at[:, mine], local.at[7])
         wait_send(G, i_s.at[5])
 
     wait_recv(out.at[:, other], i_r.at[5])
-    moved(FIND.at[s], down.at[s], local.at[9])
-    wait_send(FIND.at[t], i_s.at[6])
+    moved(lower(s), down.at[s], local.at[9])
+    wait_send(lower(t), i_s.at[6])
     wait_recv(down.at[t], i_r.at[6])
     wait_send(wd_ref.at[t], i_s.at[1])
     wait_send(gain_ref, i_s.at[2])
@@ -910,10 +982,11 @@
         wait_send(GT.at[0], gs.at[n])
     for kind in range(3):
         sent(kind)
-    staged_free(10)
-    staged_free(11)
-    for j in range(SETS):
+    wait_send(STG.at[0, pl.ds(0, 3), t], gss.at[2])
+    wait_send(STG.at[0, pl.ds(0, 3), t], gss.at[3])
+    for j in range(9):
         scattered(j)
+    G_sent()
 
 
 def finish_kernel(len_ref, pre, out, a, b, ins, outs):
@@ -949,19 +1022,19 @@
         bulk(3 * D, T), bulk(D, T), bulk(D, T), bulk(D, T), bulk(D, T),
         full(D, T), full(D, T), full(T // SLOTS, 2, TILE, TILE), full(16, T), full(8, T),
         full(2, 1, D), full(2, D, 128), full(D, 128), full(2, 1, D), full(6, 1, D), full(4, 1, D),
-        bulk(2, 4, 2, 2, 48, D), bulk(SETS, 4, 2, 48, D), bulk(SETS, 2, 2, 48, D), bulk(SETS, 2, 48, D),
-        bulk(3, 2, 48, D), bulk(4, 2, 48, D), bulk(2, 4, 48, D), full(2, 2, 48, D), full(2, 48, D),
+        bulk(2, 4, 2, 2, 48, D), bulk(2, 4, 2, 48, D), bulk(SETS, 4, 2, 48, D), bulk(SETS, 2, 2, 48, D), bulk(SETS, 2, 48, D),
+        bulk(3, 2, 48, D), bulk(4, 2, 48, D), bulk(2, 4, 48, D),
         dma(3, 4), dma(3, 4), dma(3, 4, 4), dma(3, 4, 4),
-        dma(SETS), dma(SETS), dma(SETS, 2), dma(SETS, 2), dma(SETS), dma(SETS),
+        dma(SETS, 2), dma(SETS, 2), dma(SETS, 2), dma(SETS, 2), dma(SETS), dma(SETS),
         dma(SETS, 2), dma(3), dma(4), dma(2, 4),
-        dma(8), dma(8), dma(11), dma(6), dma(6),
+        dma(8), dma(8), dma(11), dma(6), dma(6), dma(4), dma(4),
     ]
     out, first, down, gains, _, _ = pl.pallas_call(
         layer_kernel,
         in_specs=[S, V, HBM, HBM, HBM, HBM],
         out_specs=[HBM, HBM, HBM, V, HBM, HBM],
         out_shape=[
-            sds(D, 2 * T), sds(2, 2, 48, D), sds(2, 48, D), sds(1, D), sds(D, T), sds(3 * D, T, dtype=bf16),
+            sds(D, 2 * T), sds(2, 96, D), sds(2, 48, D), sds(1, D), sds(D, T), sds(3 * D, T, dtype=bf16),
         ],
         scratch_shapes=scratch,
         compiler_params=pltpu.CompilerParams(collective_id=1, has_side_effects=True, vmem_limit_bytes=VMEM_MOST),

time: 204 us -> 181 us (0.89)
  Pallas kernels: 197 us -> 173 us
    pallas_call x1, Pallas kernels: 191 us -> 168 us  [layer(): pl.pallas_call(layer_kernel, in_specs=[S, V, HBM, HBM, HBM, HBM], out_spe...]
where the time goes in v3:
time: 181 us; the launch traced here: 180 us
  Pallas kernels  173 us (96%)
  local copies, waits for them, and re-layouts  5.53 us (3%)
    pallas_call x1, Pallas kernels, layer(): pl.pallas_call(layer_kernel, in_specs=[S, V, HBM, HBM, HBM, HBM], out_spe...  168 us
    pallas_call x1, Pallas kernels, layer(): pl.pallas_call(finish_kernel, in_specs=[S, HBM], out_specs=HBM, out_shape...  5.19 us
    unnamed x10, local copies, waits for them, and re-layouts  4.32 us

profile of v3, /device:TPU:1, one launch (start us, length us, event | category | flops | bytes accessed | tf_op | source)
XLA Modules:
  0.0 179.6 jit_solution(9505790747759412126)
XLA Ops:
  0.6 0.0 copy-start.1
  0.6 168.2 %layer.1 = (f32[768,2048]{1,0:T(8,128)}, f32[2,96,768]{2,1,0:T(8,128)}, f32[2,48,768]{2,1,0:T(8,128)}, f32[1,768]{1,0:T(1,128)}, f32[768,1024]{1,0:T(8,128)}, /*index=5*/bf16[2304,1024]{1,0:T(8,128)(2,1)}) custom-call(s32[4,4]{1,0:T(4,128)} %len_ref.3, s32[1,2048]{1,0:T(1,128)} %bitcast.25, f32[1,768]{1,0:T(1,128)} %gain_ref.1, f32[767,1,2048]{2,1,0:T(1,128)} %bitcast.19, ...), custom_call_target="tpu_custom_call" | custom-call | tf_op jit(solution)/shard_map/layer/pallas_call | solution.py:1032
  168.8 0.0 copy-done.1
  168.8 0.0 copy-start
  168.8 2.8 %copy-done = f32[768,2048]{1,0:T(8,128)S(1)} copy-done((f32[768,2048]{1,0:T(8,128)S(1)}, f32[768,2048]{1,0:T(8,128)}, u32[]{:S(2)}) %copy-start) | copy-done | bytes 6291480
  171.6 0.0 copy-start.2
  171.6 0.0 copy-start.3
  171.6 5.2 %finish.1 = f32[767,1,2048]{2,1,0:T(1,128)} custom-call(s32[4,4]{1,0:T(4,128)S(1)} %copy-done.1, f32[768,2048]{1,0:T(8,128)S(1)} %copy-done), custom_call_target="tpu_custom_call" | custom-call | tf_op jit(solution)/shard_map/finish/pallas_call | solution.py:1043
  176.8 1.2 constant_dynamic-slice_fusion
  178.0 0.0 copy-done.2
  178.0 0.8 copy.12
  178.9 0.0 copy-done.3
  178.9 0.7 copy.13
Async XLA Ops:
  0.6 168.2 %copy-start.1 = (s32[4,4]{1,0:T(4,128)S(1)}, s32[4,4]{1,0:T(4,128)}, u32[]{:S(2)}) copy-start(s32[4,4]{1,0:T(4,128)} %len_ref.3) | copy-start | bytes 196
  168.8 2.8 %copy-start = (f32[768,2048]{1,0:T(8,128)S(1)}, f32[768,2048]{1,0:T(8,128)}, u32[]{:S(2)}) copy-start(f32[768,2048]{1,0:T(8,128)} %get-tuple-element.8.pre) | copy-start | bytes 18874372
  171.6 6.4 %copy-start.2 = (f32[2,96,768]{2,1,0:T(8,128)S(1)}, f32[2,96,768]{2,1,0:T(8,128)}, u32[]{:S(2)}) copy-start(f32[2,96,768]{2,1,0:T(8,128)} %get-tuple-element.10) | copy-start | bytes 1769476
  171.6 7.2 %copy-start.3 = (f32[2,48,768]{2,1,0:T(8,128)S(1)}, f32[2,48,768]{2,1,0:T(8,128)}, u32[]{:S(2)}) copy-start(f32[2,48,768]{2,1,0:T(8,128)} %get-tuple-element.11) | copy-start | bytes 884740

commit v4 on v3

--- a/solution.py
+++ b/solution.py
@@ -246,6 +246,8 @@
 
 DIST = (0, 1, 3, 2)
 CHUNKS = (0, 2, 1, 3)
+FAR_KIND = -1
+FAR_SETS = ()
 TILE = 256
 SCALE = HEAD_DIM ** -0.5
 KIND_A, KIND_D, KIND_W = 0, 1, 2
@@ -270,7 +272,7 @@
     out, first, down, gain_out, spill_x, spill_q,
     fa, fw, fd, X, G, xt, gt, QKV, ATT, H0, H1, DM, MACC, HACC, BIAS, LSE, MK, GR, GCOL, GG, GV, GL, GT,
     STG, STGD, ACC, L1, L2, L3W, L3A, L3D,
-    zs, zr, ps, pr, ss, sr, p1s, p1r, p2s, p2r, p3s, rw, ra, rd, i_s, i_r, local, gs, gr, gss, gsr,
+    zs, zr, ps, pr, ss, sr, p1s, p1r, p2s, p2r, p3s, rw, ra, rd, i_s, i_r, local, gs, gr, gss, gsr, vs, vr,
 ):
     s, d = lax.axis_index("section"), lax.axis_index("dp")
     x, y, z, xy = lax.rem(d, 2), lax.rem(d // 2, 2), d // 4, lax.rem(d, 4)
@@ -338,6 +340,8 @@
         push(here, here, ps.at[kind, i, 1], pr.at[kind, i, 1], n2)
 
     def B(kind, i):
+        if kind == FAR_KIND and i:
+            return
         here = slab(kind, plane(i, kind), xy1, s)
         wait_recv(here, pr.at[kind, i, 0])
         push(here, here, ps.at[kind, i, 2], pr.at[kind, i, 2], n2)
@@ -345,7 +349,15 @@
     def C(kind, i):
         zz = plane(i, kind)
         wait_recv(slab(kind, zz, xy2, s), pr.at[kind, i, 1])
-        wait_recv(slab(kind, zz, xy3, s), pr.at[kind, i, 2])
+        if kind == FAR_KIND and i:
+            wait_recv(slab(kind, zz, xy1, s), pr.at[kind, i, 0])
+            wait_recv(slab(kind, zz, xy3, s), vr.at[CHUNKS[i]])
+        else:
+            wait_recv(slab(kind, zz, xy3, s), pr.at[kind, i, 2])
+        if kind == FAR_KIND and i == 0:
+            far_slab = slab(kind, z, xy3, s)
+            for far in (2, 1, 3):
+                push(far_slab, far_slab, vs.at[far], vr.at[far], at_plane(lax.rem(z + far, 4)))
         here = group(kind, zz, s)
         push(here, here, ps.at[kind, i, 3], pr.at[kind, i, 3], sib)
 
@@ -359,7 +371,10 @@
                 wait_send(slab(kind, z, xy, s), zs.at[kind, i])
             wait_send(slab(kind, zz, xy, s), ps.at[kind, i, 0])
             wait_send(slab(kind, zz, xy, s), ps.at[kind, i, 1])
-            wait_send(slab(kind, zz, xy1, s), ps.at[kind, i, 2])
+            if kind == FAR_KIND and i:
+                wait_send(slab(kind, z, xy3, s), vs.at[i])
+            else:
+                wait_send(slab(kind, zz, xy1, s), ps.at[kind, i, 2])
             wait_send(group(kind, zz, s), ps.at[kind, i, 3])
 
     def to_sibling(j, slot, down_set=False):
@@ -390,13 +405,27 @@
             for q in range(4):
                 ACC[j, q] = (wide(ACC[j, q]) + wide(STG[slot_of(j), q, s])).astype(bf16)
         push(ACC.at[j, xy2], L1.at[j, 0], p1s.at[j, 0], p1r.at[j, 0], n2)
-        push(ACC.at[j, xy3], L1.at[j, 1], p1s.at[j, 1], p1r.at[j, 1], n2)
+        if j in FAR_SETS:
+            push(ACC.at[j, xy3], L1.at[j, 1], p1s.at[j, 1], p1r.at[j, 1], at_plane(plane(j // 2)))
+        elif j or not FAR_SETS:
+            push(ACC.at[j, xy3], L1.at[j, 1], p1s.at[j, 1], p1r.at[j, 1], n2)
+
+    def RD():
+        if not FAR_SETS:
+            return
+        v = wide(ACC[0, xy3])
+        for j in FAR_SETS:
+            wait_recv(L1.at[j, 1], p1r.at[j, 1])
+            v = v + wide(L1[j, 1])
+        ACC[0, xy3] = v.astype(bf16)
+        push(ACC.at[0, xy3], L1.at[0, 1], p1s.at[0, 1], p1r.at[0, 1], n2)
 
     def R2(j):
         wait_recv(L1.at[j, 0], p1r.at[j, 0])
-        wait_recv(L1.at[j, 1], p1r.at[j, 1])
         ACC[j, xy] = (wide(ACC[j, xy]) + wide(L1[j, 0])).astype(bf16)
-        ACC[j, xy1] = (wide(ACC[j, xy1]) + wide(L1[j, 1])).astype(bf16)
+        if j not in FAR_SETS:
+            wait_recv(L1.at[j, 1], p1r.at[j, 1])
+            ACC[j, xy1] = (wide(ACC[j, xy1]) + wide(L1[j, 1])).astype(bf16)
         push(ACC.at[j, xy1], L2.at[j], p2s.at[j], p2r.at[j], n1)
 
     def ends_of(j):
@@ -710,11 +739,11 @@
         H1[:, c] = (v * inv_rms(v) * GCOL[1, :, :1]).astype(bf16)
         ticks(i, {0: [(A, KIND_D, 3), (B, KIND_D, 2)], 2: [(C, KIND_W, 1)]})
 
+    A(KIND_W, 2)
+    B(KIND_D, 3)
     MACC[...] = jnp.zeros_like(MACC)
     HACC[...] = jnp.zeros_like(HACC)
     moved(QKV, spill_q, local.at[6])
-    A(KIND_W, 2)
-    B(KIND_D, 3)
     E(KIND_D, 0)
     E(KIND_D, 1)
     E(KIND_W, 0)
@@ -750,9 +779,10 @@
 
         for i in range(tiles):
             c = slice(i * TILE, (i + 1) * TILE)
-            act, slope = gelu_both(nn(square(fw[p]), H1[:, c]))
+            before, back = nn(square(fw[p]), H1[:, c]), nn(down_rows(), DM[:, c])
+            act, slope = gelu_both(before)
             ZT[:, c] = act.astype(bf16)
-            DU[:, c] = (nn(down_rows(), DM[:, c]) * slope).astype(bf16)
+            DU[:, c] = (back * slope).astype(bf16)
         tick("a")
 
         slot = lax.rem(k, 2)
@@ -989,26 +1019,34 @@
     G_sent()
 
 
-def finish_kernel(len_ref, pre, out, a, b, ins, outs):
+def finish_kernel(len_ref, pre, first, down, gain, out, first_out, down_out, gain_out, a, b, c, e, ins, outs, rest):
     n = pre.shape[1] // SLOTS
     cols = lambda i: pl.ds(i * SLOTS, SLOTS)
-    load = lambda i: pltpu.make_async_copy(pre.at[:, cols(i)], a.at[i % 2], ins.at[i % 2])
-    save = lambda i: pltpu.make_async_copy(b.at[i % 2], out.at[:, 0, cols(i)], outs.at[i % 2])
-    load(0).start()
+    load = lambda i: pltpu.make_async_copy(pre.at[:, cols(i)], a.at[i], ins.at[i])
+    save = lambda i: pltpu.make_async_copy(b.at[i], out.at[:, 0, cols(i)], outs.at[i])
+    for i in range(n):
+        load(i).start()
+    passed = ((first, c, first_out, 0), (down, e, down_out, 2))
+    for src, between, dst, at in passed:
+        pltpu.make_async_copy(src, between, rest.at[at]).start()
+    share = gain_out.shape[1]
+    back = lax.rem(D - lax.axis_index("dp") * share, D)
+    gain_out[...] = pltpu.roll(jnp.broadcast_to(gain[...], (8, D)), back, 1)[:1, :share]
     for i in range(n):
         load(i).wait()
-        if i + 1 < n:
-            load(i + 1).start()
         start, shift = 0, 0
         for j in range(4):
             shift = shift + jnp.where(len_ref[i, j] == LONGEST, start, 0)
             start = start + len_ref[i, j]
-        if i >= 2:
-            save(i - 2).wait()
-        b[i % 2] = pltpu.roll(a[i % 2], shift, 1)[:D - 1]
+        b[i] = pltpu.roll(a[i], shift, 1)[:D - 1]
         save(i).start()
-    for i in range(max(n - 2, 0), n):
+    for src, between, dst, at in passed:
+        pltpu.make_async_copy(src, between, rest.at[at]).wait()
+        pltpu.make_async_copy(between, dst, rest.at[at + 1]).start()
+    for i in range(n):
         save(i).wait()
+    for src, between, dst, at in passed:
+        pltpu.make_async_copy(between, dst, rest.at[at + 1]).wait()
 
 
 def layer(lengths, mask, gain, stream, w, wd):
@@ -1027,7 +1065,7 @@
         dma(3, 4), dma(3, 4), dma(3, 4, 4), dma(3, 4, 4),
         dma(SETS, 2), dma(SETS, 2), dma(SETS, 2), dma(SETS, 2), dma(SETS), dma(SETS),
         dma(SETS, 2), dma(3), dma(4), dma(2, 4),
-        dma(8), dma(8), dma(11), dma(6), dma(6), dma(4), dma(4),
+        dma(8), dma(8), dma(11), dma(6), dma(6), dma(4), dma(4), dma(4), dma(4),
     ]
     out, first, down, gains, _, _ = pl.pallas_call(
         layer_kernel,
@@ -1040,15 +1078,16 @@
         compiler_params=pltpu.CompilerParams(collective_id=1, has_side_effects=True, vmem_limit_bytes=VMEM_MOST),
         name="layer",
     )(lengths, mask, gain, stream, w.reshape(2, 96, D), wd.reshape(2, 48, D))
-    final = pl.pallas_call(
+    share = D // lax.axis_size("dp")
+    final, first, down, gains = pl.pallas_call(
         finish_kernel,
-        in_specs=[S, HBM],
-        out_specs=HBM,
-        out_shape=sds(D - 1, 1, 2 * T),
-        scratch_shapes=[full(2, D, SLOTS), full(2, D - 1, SLOTS), dma(2), dma(2)],
-        compiler_params=pltpu.CompilerParams(vmem_limit_bytes=32 * 2**20),
+        in_specs=[S, HBM, HBM, HBM, V],
+        out_specs=[HBM, HBM, HBM, V],
+        out_shape=[sds(D - 1, 1, 2 * T), sds(2, 96, D), sds(2, 48, D), sds(1, share)],
+        scratch_shapes=[full(4, D, SLOTS), full(4, D - 1, SLOTS), full(2, 96, D), full(2, 48, D), dma(4), dma(4), dma(4)],
+        compiler_params=pltpu.CompilerParams(vmem_limit_bytes=VMEM_MOST),
         name="finish",
-    )(lengths, out)
+    )(lengths, out, first, down, gains)
     return final, first.reshape(192, D), down.reshape(96, D), gains
 
 
@@ -1088,13 +1127,13 @@
     w = jnp.transpose(first_proj[0])
     wd = jnp.transpose(down_proj)
     if sizes == (2, 16) and stream.shape[2] == 4 * SLOTS:
-        out, first, down, gain_total = layer(doc_lengths, pad_mask[None], norm_gains, stream, w, wd)
+        out, first, down, gain_share = layer(doc_lengths, pad_mask[None], norm_gains, stream, w, wd)
     else:
         out, first, down, gain_total = separate(
             own, stream, w, wd, norm_gains, doc_lengths, pad_mask, sections, groups
         )
-    share = D // groups
-    gain_share = lax.dynamic_slice_in_dim(gain_total, own[1] * share, share, axis=1)
+        share = D // groups
+        gain_share = lax.dynamic_slice_in_dim(gain_total, own[1] * share, share, axis=1)
     return jnp.transpose(out, (1, 2, 0)), gain_share, jnp.transpose(first)[None], jnp.transpose(down)
 
 

time: 181 us -> 177 us (0.978)
  local copies, waits for them, and re-layouts: 5.53 us -> 0 us
  Pallas kernels: 173 us -> 175 us
    unnamed x10 -> x0, local copies, waits for them, and re-layouts: 4.32 us -> none
where the time goes in v4:
time: 177 us; the launch traced here: 176 us
  Pallas kernels  175 us (99%)
    pallas_call x1, Pallas kernels, layer(): pl.pallas_call(layer_kernel, in_specs=[S, V, HBM, HBM, HBM, HBM], out_spe...  168 us
    pallas_call x1, Pallas kernels, layer(): pl.pallas_call(finish_kernel, in_specs=[S, HBM, HBM, HBM, V], out_specs=[...  6.46 us

profile of v4, /device:TPU:1, one launch (start us, length us, event | category | flops | bytes accessed | tf_op | source)
XLA Modules:
  0.0 175.6 jit_solution(13161761238093091378)
XLA Ops:
  0.6 168.3 %layer.1 = (f32[768,2048]{1,0:T(8,128)}, f32[2,96,768]{2,1,0:T(8,128)}, f32[2,48,768]{2,1,0:T(8,128)}, f32[1,768]{1,0:T(1,128)}, f32[768,1024]{1,0:T(8,128)}, /*index=5*/bf16[2304,1024]{1,0:T(8,128)(2,1)}) custom-call(s32[4,4]{1,0:T(4,128)} %len_ref.3, s32[1,2048]{1,0:T(1,128)} %bitcast.22, f32[1,768]{1,0:T(1,128)} %gain_ref.1, f32[767,1,2048]{2,1,0:T(1,128)} %bitcast.19, ...), custom_call_target="tpu_custom_call" | custom-call | tf_op jit(solution)/shard_map/layer/pallas_call | solution.py:1070
  169.0 6.5 %finish.1 = (f32[767,1,2048]{2,1,0:T(1,128)}, f32[2,96,768]{2,1,0:T(8,128)}, f32[2,48,768]{2,1,0:T(8,128)}, f32[1,48]{1,0:T(1,128)}) custom-call(s32[4,4]{1,0:T(4,128)} %len_ref.3, f32[768,2048]{1,0:T(8,128)} %get-tuple-element.12.pre, f32[2,96,768]{2,1,0:T(8,128)} %get-tuple-element.13.first, f32[2,48,768]{2,1,0:T(8,128)} %get-tuple-element.14.down, ...), custom_call_target="tpu_custom_call" | custom-call | tf_op jit(solution)/shard_map/finish/pallas_call | solution.py:1082
